TPU v7x, 512 devices: a whole 4x4x16 slice. The times are simulated.
512 devices in a mesh: blk: 32 (over z, core), grp: 16 (over x, y).
Axes of the slice: x: 4, y: 4, z: 16, core: 2. Of those that a mesh axis runs over, the one named last changes fastest.
Arguments:
- signal: bfloat16 [16, 64, 16384], P('grp', None, 'blk'), may hold values from -10 to 10
- lag_table: int32 [512], replicated, may hold values from 0 to 511, each once
- window_end: int32 [16, 32], P('grp', 'blk'), may hold values from 128 to 512
Outputs:
- factors: float32 [16, 512, 512], P('grp', 'blk')
- coeffs: float32 [16, 512, 64], P('grp', 'blk')
- residual: float32 [16, 64, 16384], P('grp', None, 'blk')
Inputs may be any that keep to these rules, and one draw needn't show every extreme that they name: `lag_table`: each of 0 to 511 appears once.
All inputs are finite; a program needn't handle non-finite values.
Results may differ from a plain program's by a relative error of at most 0.0003.
Values may be sent and summed in bfloat16 or wider, within the bound.
No kernel may reach another device: no remote copies, remote signals or barrier semaphores. Data moves between devices by JAX's collectives and lax.ppermute only.
A program may use at most 192 MiB of HBM per device.

v0:
```python
import math

import jax
import jax.numpy as jnp
from jax import lax
from jax.sharding import PartitionSpec as P

ridge_weight = 4.0


def passed_along(block, axis, distance):
    devices = range(lax.axis_size(axis))
    route = [((i - distance) % len(devices), i) for i in devices]
    return lax.ppermute(block, axis, route)


def passed_along_2(block, axis, distance):
    devices = range(lax.axis_size(axis))
    route = [(i - distance, i) for i in devices if i - distance in devices]
    return lax.ppermute(block, axis, route)


def entering(x, axis, combine, identity):
    peers, index = (lax.axis_size(axis), lax.axis_index(axis))
    everything = jax.tree.map(lambda part: lax.all_gather(part, axis), x)
    start = jax.tree.map(
        lambda part, zero: jnp.broadcast_to(jnp.asarray(zero, part.dtype), part.shape), x, identity
    )

    def step(k, before):
        reached = k < index
        new = combine(before, jax.tree.map(lambda part: part[k], everything))
        return jax.tree.map(lambda a, b: jnp.where(reached, a, b), new, before)

    return lax.fori_loop(0, peers, step, start)


def lagged_block(history, row_start, block_len, lag_count):
    pieces = [
        lax.dynamic_slice_in_dim(history, row_start + (lag_count - 1 - delay_index), block_len, 1)
        for delay_index in range(lag_count)
    ]
    return jnp.concatenate(pieces, axis=0)


def highest(first_matrix, second_matrix):
    return jnp.dot(first_matrix, second_matrix, precision=lax.Precision.HIGHEST)


def contract_time(first_matrix, second_matrix):
    return lax.dot_general(
        first_matrix, second_matrix, (((1,), (1,)), ((), ())), preferred_element_type=jnp.float32
    )


def upper_of(gram_part):
    return jnp.linalg.cholesky(gram_part).T


def add_pairs(earlier_part, later_part):
    return (earlier_part[0] + later_part[0], earlier_part[1] + later_part[1])


def on_device(signal, lag_table, window_end):
    series = signal[0]
    sensor_count, row_count = series.shape
    col_count = lag_table.shape[0]
    lag_count = col_count // sensor_count
    block_len = min(512, row_count)
    block_count = row_count // block_len
    tail_cols = series[:, row_count - lag_count :]
    prior_cols = passed_along(tail_cols, "blk", 1)
    earlier_cols = passed_along_2(prior_cols, "grp", 1)
    rim_cols = jnp.where(lax.axis_index("blk") == 0, earlier_cols, prior_cols)
    history = jnp.concatenate([rim_cols, series], axis=1)
    end_row = window_end[0, 0]

    def accumulate(step_index, carry_pair):
        gram_part, cross_part = carry_pair
        row_start = step_index * block_len
        lagged = lagged_block(history, row_start, block_len, lag_count)
        target = lax.dynamic_slice_in_dim(history, row_start + lag_count, block_len, 1)
        live_mask = row_start + jnp.arange(block_len, dtype=jnp.int32) < end_row
        masked = jnp.where(live_mask[None, :], lagged, jnp.zeros_like(lagged))
        return (
            gram_part + contract_time(masked, lagged),
            cross_part + contract_time(masked, target),
        )

    start_gram = ridge_weight * jnp.eye(col_count, dtype=jnp.float32)
    start_cross = jnp.zeros((col_count, sensor_count), jnp.float32)
    gram_sum, cross_sum = lax.fori_loop(0, block_count, accumulate, (start_gram, start_cross))
    gram_sum = gram_sum[lag_table][:, lag_table]
    cross_sum = cross_sum[lag_table]
    group_gram, cross_sum = lax.psum((gram_sum, cross_sum), "blk")
    identity = (jnp.zeros_like(group_gram), jnp.zeros_like(cross_sum))
    earlier_part = entering((group_gram, cross_sum), "grp", add_pairs, identity)
    prefix_gram, prefix_cross = add_pairs(earlier_part, (group_gram, cross_sum))
    prefix_factor = upper_of(prefix_gram)
    lower_factor = prefix_factor.T
    half_solved = lax.linalg.triangular_solve(
        lower_factor, prefix_cross, left_side=True, lower=True
    )
    coefficients = lax.linalg.triangular_solve(
        lower_factor, half_solved, left_side=True, lower=True, transpose_a=True
    )
    share_rows = col_count // lax.axis_size("blk")
    first_row = lax.axis_index("blk") * share_rows
    factor_rows = lax.dynamic_slice_in_dim(prefix_factor, first_row, share_rows, 0) / math.sqrt(
        row_count * lax.axis_size("blk")
    )
    coef_rows = lax.dynamic_slice_in_dim(coefficients, first_row, share_rows, 0)
    canonical = jnp.zeros_like(coefficients).at[lag_table].set(coefficients)

    def residual_step(step_index, output):
        row_start = step_index * block_len
        lagged = lagged_block(history, row_start, block_len, lag_count).astype(jnp.float32)
        target = lax.dynamic_slice_in_dim(history, row_start + lag_count, block_len, 1).astype(
            jnp.float32
        )
        fitted = highest(canonical.T, lagged)
        return lax.dynamic_update_slice_in_dim(output, target - fitted, row_start, 1)

    residual = lax.fori_loop(
        0, block_count, residual_step, jnp.zeros((sensor_count, row_count), jnp.float32)
    )
    return (factor_rows[None], coef_rows[None], residual[None])


def solution(mesh):
    return jax.shard_map(
        on_device,
        mesh=mesh,
        in_specs=(P("grp", None, "blk"), P(), P("grp", "blk")),
        out_specs=(P("grp", "blk", None), P("grp", "blk", None), P("grp", None, "blk")),
        check_vma=False,
    )
```

profile of v0, /device:TPU:1, one launch (start us, length us, event | category | flops | bytes accessed | tf_op | source)
XLA Modules:
  0.0 646.3 jit_solution(2128544123840984766)
XLA Ops:
  8.0 3.0 collective-permute-start
  12.4 3.2 collective-permute-done
  29.1 2.3 gather_fusion.1
  31.4 1.6 gather_fusion.2
  33.1 218.0 %all-reduce.4.cloned.1.call-done = (f32[512,512]{0,1:T(8,128)}, f32[512,64]{1,0:T(8,128)}) async-done(((f32[512,512]{0,1:T(8,128)}, f32[512,64]{1,0:T(8,128)}), (f32[512,512]{0,1:T(8,128)}, f32[512,64]{1,0:T(8,128)})) %all-reduce.4.cloned.1.call-update) | async-done | bytes 1179664 | tf_op jit(solution)/shard_map/psum | solution.py:95
  251.9 129.1 %all-gather.5.cloned.1.call-done = f32[8192,512]{0,1:T(8,128)} async-done(((f32[512,512]{0,1:T(8,128)}), f32[8192,512]{0,1:T(8,128)}) %all-gather.5.cloned.1.call-update) | async-done | bytes 16777232 | tf_op jit(solution)/shard_map/all_gather | solution.py:25
  381.0 17.5 %copy.29 = f32[8192,512]{1,0:T(8,128)} copy(f32[8192,512]{0,1:T(8,128)} %all-gather.5.cloned.1.call-done) | data formatting | bytes 33554432
  398.5 52.7 %all-gather.7.cloned.1.call-done = f32[8192,64]{1,0:T(8,128)} async-done(((f32[512,64]{1,0:T(8,128)}), f32[8192,64]{1,0:T(8,128)}) %all-gather.7.cloned.1.call-update) | async-done | bytes 2097168 | tf_op jit(solution)/shard_map/all_gather | solution.py:25
  451.1 42.5 %while.12 = (s32[]{:T(128)}, f32[512,512]{1,0:T(8,128)S(1)}, f32[512,64]{1,0:T(8,128)S(1)}, s32[]{:T(128)}, f32[16,512,512]{2,1,0:T(8,128)}, /*index=5*/f32[16,512,64]{2,1,0:T(8,128)}, s32[]{:T(128)}, s32[]{:T(128)}) while((s32[]{:T(128)}, f32[512,512]{1,0:T(8,128)S(1)}, f32[512,64]{1,0:T(8,128)S(1)}, s32[]{:T(128)}, ...), condition=%wide.region_3.4_spmd.clone, body=%wide.region_2.3_spmd.clone.sunk | while | flops 884740 | bytes 3539059 | solution.py:35
  494.8 11.7 %cholesky.103 = f32[128,128]{1,0:T(8,128)S(1)} custom-call(f32[128,128]{1,0:T(8,128)S(1)} %cholesky.263), custom_call_target="Cholesky" | custom-call | tf_op jit(solution)/shard_map/jit(cholesky)/cholesky | solution.py:57
  506.6 9.8 %custom-call.32 = f32[1,128,128]{1,2,0:T(8,128)S(1)} custom-call(f32[1,128,128]{2,1,0:T(8,128)S(1)} %get-tuple-element.230), custom_call_target="InvertDiagBlocksLowerTriangular" | custom-call | tf_op jit(solution)/shard_map/jit(cholesky)/cholesky | solution.py:57
  517.6 11.7 %cholesky.215 = f32[128,128]{1,0:T(8,128)S(1)} custom-call(f32[128,128]{1,0:T(8,128)S(1)} %cholesky.267), custom_call_target="Cholesky" | custom-call | tf_op jit(solution)/shard_map/jit(cholesky)/cholesky | solution.py:57
  529.3 10.0 %custom-call.33 = f32[1,128,128]{1,2,0:T(8,128)S(1)} custom-call(f32[1,128,128]{2,1,0:T(8,128)S(1)} %get-tuple-element.227), custom_call_target="InvertDiagBlocksLowerTriangular" | custom-call | tf_op jit(solution)/shard_map/jit(cholesky)/cholesky | solution.py:57
  540.0 11.7 %cholesky.236 = f32[128,128]{1,0:T(8,128)S(1)} custom-call(f32[128,128]{1,0:T(8,128)S(1)} %cholesky.272), custom_call_target="Cholesky" | custom-call | tf_op jit(solution)/shard_map/jit(cholesky)/cholesky | solution.py:57
  552.5 9.8 %custom-call.34 = f32[1,128,128]{1,2,0:T(8,128)S(1)} custom-call(f32[1,128,128]{2,1,0:T(8,128)S(1)} %get-tuple-element.224), custom_call_target="InvertDiagBlocksLowerTriangular" | custom-call | tf_op jit(solution)/shard_map/jit(cholesky)/cholesky | solution.py:57
  562.9 11.9 %cholesky.253 = f32[128,128]{1,0:T(8,128)S(1)} custom-call(f32[128,128]{1,0:T(8,128)S(1)} %convolution_subtract_fusion.6), custom_call_target="Cholesky" | custom-call | tf_op jit(solution)/shard_map/jit(cholesky)/cholesky | solution.py:57
  578.9 10.4 %while.11 = (s32[]{:T(128)}, f32[512,512]{1,0:T(8,128)S(1)}, s32[4,2]{0,1:T(2,128)S(1)}, f32[4,128,128]{2,1,0:T(8,128)}, s32[]{:T(128)}) while((s32[]{:T(128)}, f32[512,512]{1,0:T(8,128)S(1)}, s32[4,2]{0,1:T(2,128)S(1)}, f32[4,128,128]{2,1,0:T(8,128)}, s32[]{:T(128)}) %tuple.69), condition=%wide.while_cond, body=%wide.while_body.sunk | while | flops 2 | bytes 132705 | solution.py:104
  579.5 2.0 bitcast_dynamic-update-slice_fusion.2
  582.1 2.0 bitcast_dynamic-update-slice_fusion.2
  584.7 2.0 bitcast_dynamic-update-slice_fusion.2
  587.3 2.0 bitcast_dynamic-update-slice_fusion.2
  589.3 40.1 %custom-call.35 = f32[4,128,128]{1,2,0:T(8,128)S(1)} custom-call(f32[4,128,128]{2,1,0:T(8,128)} %get-tuple-element.155), custom_call_target="InvertDiagBlocksLowerTriangular" | custom-call | tf_op jit(solution)/shard_map/triangular_solve | solution.py:104
  634.2 1.8 scatter_custom_fusion
  636.0 2.1 fusion
  (121 shorter events, 72.2 us)
Async XLA Ops:
  7.2 243.9 %all-reduce.4.cloned.1.call-start = ((), (), s32[]{:S(2)}) async-start(), calls=%async_computation.2 | async-start | bytes 2621440 | tf_op jit(solution)/shard_map/psum | solution.py:95
  8.0 7.6 %collective-permute-start = (bf16[64,8]{1,0:T(8,128)(2,1)S(1)}, bf16[64,8]{1,0:T(8,128)(2,1)S(1)}, u32[]{:S(2)}, u32[]{:S(2)}) collective-permute-start(bf16[64,8]{1,0:T(8,128)(2,1)S(1)} %slice.155), channel_id=1, source_target_pairs={{496,0},{0,16},{16,32},{32,48},{48,64},{64,80},{80,96},{96,112},{1... | collective-permute-start | bytes 3080 | tf_op jit(solution)/shard_map/ppermute | solution.py:14
  15.6 2.1 collective-permute-start.1
  25.2 0.8 copy-start.2
  33.1 347.9 %all-gather.5.cloned.1.call-start = ((), (), s32[]{:S(2)}) async-start(), calls=%async_computation | async-start | bytes 17825792 | tf_op jit(solution)/shard_map/all_gather | solution.py:25
  251.1 200.0 %all-gather.7.cloned.1.call-start = ((), (), s32[]{:S(2)}) async-start(), calls=%async_computation.1 | async-start | bytes 4456448 | tf_op jit(solution)/shard_map/all_gather | solution.py:25
  398.4 95.6 %copy-start.1 = (f32[512,512]{0,1:T(8,128)S(1)}, f32[512,512]{0,1:T(8,128)}, u32[]{:S(2)}) copy-start(f32[512,512]{0,1:T(8,128)} %get-tuple-element.215) | copy-start | bytes 3145732
  493.6 142.4 %copy-start = (bf16[1,64,512]{2,1,0:T(8,128)(2,1)S(1)}, bf16[1,64,512]{2,1,0:T(8,128)(2,1)}, u32[]{:S(2)}) copy-start(bf16[1,64,512]{2,1,0:T(8,128)(2,1)} %param.5) | copy-start | bytes 196612
Sparse Core Ops, SparseCore 0:
  33.2 217.8 all-reduce.3
  254.6 126.3 all-gather.4
  384.4 66.6 all-gather.6
where the time goes:
time: 648 us; the launch traced here: 646 us
  waiting for transfers between devices  404 us (62%)
  other arithmetic  171 us (26%)
  local copies, waits for them, and re-layouts  39.2 us (6%)
  between operations  17.4 us (3%)
  matrix products  9.35 us (1%)
    psum x1, waiting for transfers between devices, on_device(): group_gram, cross_sum = lax.psum((gram_sum, cross_sum), 'blk')  218 us
    all_gather x2, waiting for transfers between devices, entering(): everything = jax.tree.map(lambda part: lax.all_gather(part, axis), x)  182 us
    another operation x14, other arithmetic, upper_of(): return jnp.linalg.cholesky(gram_part).T  78.8 us
    select_n x32, other arithmetic, step(): return jax.tree.map(lambda a, b: jnp.where(reached, a, b), new, before)  41.9 us
    another operation x4, other arithmetic, on_device(): lax.linalg.triangular_solve(lower_factor, half_solved, left_side=True, lo...  40.4 us
    unnamed x8, local copies, waits for them, and re-layouts  18.5 us
  transfers between devices with their start and end apart: 5, of which 5 were waited for; matrix products, arithmetic and copies ran while one was open for 3% of the time, Pallas kernels for 0%

commit v1 on v0

v1 whole, which is shorter than its diff:
```python
import jax
import jax.numpy as jnp
from jax import lax
from jax.experimental import pallas as pl
from jax.experimental.pallas import tpu as pltpu
from jax.sharding import PartitionSpec as P

F32 = jnp.float32
BF16 = jnp.bfloat16
RIDGE = 4.0
SENSORS = 64
LAGS = 8
COLS = 512
ROWS = 512
TILE = 128
NT = COLS // TILE
TILES = [(k, j) for k in range(NT) for j in range(k, NT)]
PACKED = (len(TILES) + NT // 2) * TILE
VMEM = pl.BlockSpec(memory_space=pltpu.VMEM)
SMEM = pl.BlockSpec(memory_space=pltpu.SMEM)


def dot(a, b, ca, cb, precision=None):
    return lax.dot_general(
        a, b, (((ca,), (cb,)), ((), ())), precision=precision, preferred_element_type=F32
    )


def gram_kernel(end_ref, table_ref, tail_ref, x_ref, lagged_ref, packed_ref):
    x = x_ref[...]
    ext = jnp.concatenate([tail_ref[...], x], axis=1).astype(F32)
    pieces = [pltpu.roll(ext, d, 1)[:, TILE:].astype(BF16) for d in range(1, LAGS + 1)]
    canonical = jnp.concatenate(pieces, axis=0)
    pair = lax.broadcasted_iota(jnp.int32, (COLS, COLS), 0)
    chosen = jnp.where(pair == table_ref[...], 1.0, 0.0).astype(BF16)
    lagged = dot(chosen, canonical, 0, 0).astype(BF16)
    lagged_ref[...] = lagged
    time = lax.broadcasted_iota(jnp.int32, (COLS, ROWS), 1)
    masked = jnp.where(time < end_ref[0, 0], lagged.astype(F32), 0.0).astype(BF16)
    eye = (
        lax.broadcasted_iota(jnp.int32, (TILE, TILE), 0)
        == lax.broadcasted_iota(jnp.int32, (TILE, TILE), 1)
    )
    ridge = jnp.where(eye, RIDGE, 0.0)
    n = 0
    for k in range(NT):
        rows = masked[k * TILE : (k + 1) * TILE]
        block = dot(rows, lagged[k * TILE :], 1, 1)
        for j in range(k, NT):
            tile = block[:, (j - k) * TILE : (j - k + 1) * TILE]
            packed_ref[n * TILE : (n + 1) * TILE, :] = tile + ridge if j == k else tile
            n += 1
    cross = dot(masked, x, 1, 1)
    half = COLS // 2
    packed_ref[n * TILE :, :] = jnp.concatenate([cross[:half], cross[half:]], axis=1)


def factor_tile(d_rows):
    n = len(d_rows)
    lane = lax.broadcasted_iota(jnp.int32, (8, TILE), 1)
    sub = lax.broadcasted_iota(jnp.int32, (8, TILE), 0)
    d = list(d_rows)
    x = [jnp.where(lane == 8 * q + sub, 1.0, 0.0) for q in range(n)]

    def col(v, c):
        return jnp.broadcast_to(v[:, c : c + 1], (8, TILE))

    def row(v, i):
        return jnp.broadcast_to(v[i : i + 1, :], (8, TILE))

    for p in range(n):
        base = 8 * p
        c = [col(d[p], base + j) for j in range(8)]
        s = {(i, j): row(c[j], i) for j in range(8) for i in range(j + 1)}
        r = [row(d[p], i) for i in range(8)]
        xr = [row(x[p], i) for i in range(8)]
        cn = [col(d[p + 1], base + j) for j in range(8)] if p + 1 < n else []
        u = {}
        inv = []
        for k in range(8):
            w = lax.rsqrt(s[k, k])
            inv.append(w)
            for j in range(k + 1, 8):
                u[k, j] = s[k, j] * w
            for i in range(k + 1, 8):
                for j in range(i, 8):
                    s[i, j] = s[i, j] - u[k, i] * u[k, j]
            r[k] = r[k] * w
            xr[k] = xr[k] * w
            if cn:
                cn[k] = cn[k] * w
            for i in range(k + 1, 8):
                r[i] = r[i] - u[k, i] * r[k]
                xr[i] = xr[i] - u[k, i] * xr[k]
                if cn:
                    cn[i] = cn[i] - u[k, i] * cn[k]
        if p + 1 < n:
            t = [cn[i] * r[i] for i in range(8)]
            d[p + 1] = d[p + 1] - (((t[0] + t[1]) + (t[2] + t[3])) + ((t[4] + t[5]) + (t[6] + t[7])))
            t = [cn[i] * xr[i] for i in range(8)]
            x[p + 1] = x[p + 1] - (((t[0] + t[1]) + (t[2] + t[3])) + ((t[4] + t[5]) + (t[6] + t[7])))
        if p + 2 < n:
            z = list(r)
            xz = list(xr)
            for k in reversed(range(8)):
                z[k] = z[k] * inv[k]
                xz[k] = xz[k] * inv[k]
                for i in range(k):
                    z[i] = z[i] - u[i, k] * z[k]
                    xz[i] = xz[i] - u[i, k] * xz[k]
            for q in range(p + 2, n):
                cq = [col(d[q], base + j) for j in range(8)]
                t = [cq[i] * z[i] for i in range(8)]
                d[q] = d[q] - (((t[0] + t[1]) + (t[2] + t[3])) + ((t[4] + t[5]) + (t[6] + t[7])))
                t = [cq[i] * xz[i] for i in range(8)]
                x[q] = x[q] - (((t[0] + t[1]) + (t[2] + t[3])) + ((t[4] + t[5]) + (t[6] + t[7])))
        du, dx = r[0], xr[0]
        for i in range(1, 8):
            du = jnp.where(sub == i, r[i], du)
            dx = jnp.where(sub == i, xr[i], dx)
        d[p] = jnp.where(lane >= base + sub, du, 0.0)
        x[p] = dx
    return d, x


def fit_kernel(blk_ref, packed_ref, lagged_ref, x_ref, factor_ref, coef_ref, resid_ref, u_ref, i_ref, w_ref):
    high = lax.Precision.HIGHEST
    half = COLS // 2
    tiles = {}
    for n, (k, j) in enumerate(TILES):
        tiles[k, j] = (n * TILE,)
    base = len(TILES) * TILE
    g = {kj: packed_ref[at : at + TILE, :] for kj, (at,) in tiles.items()}
    b = []
    for k in range(NT):
        at = base + (k * TILE) % half
        lo = (k * TILE // half) * SENSORS
        b.append(packed_ref[at : at + TILE, lo : lo + SENSORS])
    u_ref[...] = jnp.zeros_like(u_ref)
    y = []
    for k in range(NT):
        d, xi = factor_tile([g[k, k][8 * q : 8 * q + 8] for q in range(TILE // 8)])
        ukk = jnp.concatenate(d, axis=0)
        xkk = jnp.concatenate(xi, axis=0)
        i_ref[k * TILE : (k + 1) * TILE, :] = xkk
        u_ref[k * TILE : (k + 1) * TILE, k * TILE : (k + 1) * TILE] = ukk
        panel = {}
        for j in range(k + 1, NT):
            panel[j] = dot(xkk, g[k, j], 1, 0, high)
            u_ref[k * TILE : (k + 1) * TILE, j * TILE : (j + 1) * TILE] = panel[j]
        y.append(dot(xkk, b[k], 1, 0, high))
        for i in range(k + 1, NT):
            for j in range(i, NT):
                g[i, j] = g[i, j] - dot(panel[i], panel[j], 0, 0, high)
            b[i] = b[i] - dot(panel[i], y[k], 0, 0, high)
    w = [None] * NT
    for k in reversed(range(NT)):
        acc = y[k]
        for j in range(k + 1, NT):
            ukj = u_ref[k * TILE : (k + 1) * TILE, j * TILE : (j + 1) * TILE]
            acc = acc - dot(ukj, w[j], 1, 0, high)
        w[k] = dot(i_ref[k * TILE : (k + 1) * TILE, :], acc, 0, 0, high)
        w_ref[k * TILE : (k + 1) * TILE, :] = w[k]
    share = factor_ref.shape[0]
    first = pl.multiple_of(blk_ref[0, 0] * share, 8)
    factor_ref[...] = u_ref[pl.ds(first, share), :] * (1.0 / 128.0)
    coef_ref[...] = w_ref[pl.ds(first, share), :]
    wt = jnp.concatenate([w_ref[...], jnp.zeros((COLS, TILE - SENSORS), F32)], axis=1).T[:SENSORS]
    hi = wt.astype(BF16)
    rest = wt - hi.astype(F32)
    mid = rest.astype(BF16)
    low = (rest - mid.astype(F32)).astype(BF16)
    parts = dot(jnp.concatenate([hi, mid, low], axis=0), lagged_ref[...], 1, 0)
    fitted = parts[:SENSORS] + (parts[SENSORS : 2 * SENSORS] + parts[2 * SENSORS :])
    resid_ref[...] = x_ref[...].astype(F32) - fitted


def on_device(signal, lag_table, window_end):
    blks, grps = lax.axis_size("blk"), lax.axis_size("grp")
    blk, grp = lax.axis_index("blk"), lax.axis_index("grp")
    x = signal[0]
    order = lambda b, g: b * grps + g
    following = [
        (order(b, g), order(b + 1, g) if b + 1 < blks else order(0, g + 1))
        for b in range(blks)
        for g in range(grps)
        if b + 1 < blks or g + 1 < grps
    ]
    tail = lax.ppermute(x[:, ROWS - TILE :], ("blk", "grp"), following)
    lagged, packed = pl.pallas_call(
        gram_kernel,
        out_shape=[
            jax.ShapeDtypeStruct((COLS, ROWS), BF16),
            jax.ShapeDtypeStruct((PACKED, TILE), F32),
        ],
        in_specs=[SMEM, VMEM, VMEM, VMEM],
        out_specs=[VMEM, VMEM],
        compiler_params=pltpu.CompilerParams(vmem_limit_bytes=40 << 20),
    )(window_end, lag_table[None, :], tail, x)

    core, low, high = 2, 4, blks // 8
    at = lambda h, l, c: (h * low + l) * core + c
    near = [[at(h, l, c) for l in range(low)] for h in range(high) for c in range(core)]
    far = [[at(h, l, c) for h in range(high)] for l in range(low) for c in range(core)]
    other = [(i, i ^ 1) for i in range(blks)]
    c_index = blk % 2

    def swap(part, groups):
        return lax.all_to_all(part, "blk", 0, 0, axis_index_groups=groups)

    share = PACKED // blks
    parts = packed.reshape(core, low, high, share, TILE)
    mine = lax.dynamic_index_in_dim(parts, c_index, 0, keepdims=False)
    theirs = lax.dynamic_index_in_dim(parts, 1 - c_index, 0, keepdims=False)
    mine = mine + lax.ppermute(theirs, "blk", other)
    mine = swap(mine, near).sum(0)
    mine = swap(mine, far).sum(0)
    groups = lax.all_to_all(jnp.broadcast_to(mine[None], (grps, share, TILE)), "grp", 0, 0)
    until = (jnp.arange(grps) <= grp)[:, None, None]
    mine = jnp.where(until, groups, 0.0).sum(0)
    mine = swap(jnp.broadcast_to(mine[None], (high, share, TILE)), far)
    mine = swap(jnp.broadcast_to(mine[None], (low, high, share, TILE)), near)
    theirs = lax.ppermute(mine, "blk", other)
    first = jnp.where(c_index == 0, mine, theirs)
    second = jnp.where(c_index == 0, theirs, mine)
    prefix = jnp.stack([first, second]).reshape(PACKED, TILE)

    out_rows = COLS // blks
    factor, coef, resid = pl.pallas_call(
        fit_kernel,
        out_shape=[
            jax.ShapeDtypeStruct((out_rows, COLS), F32),
            jax.ShapeDtypeStruct((out_rows, SENSORS), F32),
            jax.ShapeDtypeStruct((SENSORS, ROWS), F32),
        ],
        in_specs=[SMEM, VMEM, VMEM, VMEM],
        out_specs=[VMEM, VMEM, VMEM],
        scratch_shapes=[
            pltpu.VMEM((COLS, COLS), F32),
            pltpu.VMEM((COLS, TILE), F32),
            pltpu.VMEM((COLS, SENSORS), F32),
        ],
        compiler_params=pltpu.CompilerParams(vmem_limit_bytes=40 << 20),
    )(blk.reshape(1, 1), prefix, lagged, x)
    return factor[None], coef[None], resid[None]


def solution(mesh):
    return jax.shard_map(
        on_device,
        mesh=mesh,
        in_specs=(P("grp", None, "blk"), P(), P("grp", "blk")),
        out_specs=(P("grp", "blk", None), P("grp", "blk", None), P("grp", None, "blk")),
        check_vma=False,
    )
```

time: 648 us -> 128 us (0.20)
  waiting for transfers between devices: 404 us -> 13.7 us
  other arithmetic: 171 us -> 0.28 us
  blocking collectives: 0 us -> 63.9 us
  local copies, waits for them, and re-layouts: 39.2 us -> 1.63 us
  Pallas kernels: 0 us -> 22.5 us
  starting transfers between devices: 4.42 us -> 23.6 us
  between operations: 17.4 us -> 1.43 us
  matrix products: 9.35 us -> 0 us
    psum x1 -> x0, waiting for transfers between devices: 218 us -> none  [on_device(): group_gram, cross_sum = lax.psum((gram_sum, cross_sum), 'blk')]
    all_gather x2 -> x0, waiting for transfers between devices: 182 us -> none  [entering(): everything = jax.tree.map(lambda part: lax.all_gather(part, axis), x)]
    another operation x18 -> x2, other arithmetic: 119 us -> 0.11 us  [on_device(): prefix = jnp.stack([first, second]).reshape(PACKED, TILE)]
    all_to_all x0 -> x4, blocking collectives: none -> 63.9 us  [swap(): return lax.all_to_all(part, 'blk', 0, 0, axis_index_groups=groups)]
    select_n x34 -> x0, other arithmetic: 42.6 us -> none  [the longest x32 41.9 us: step(): return jax.tree.map(lambda a, b: jnp.where(reached, a, b), new, before)]
    pallas_call x0 -> x2, Pallas kernels: none -> 22.5 us  [the longest x1 21.2 us: on_device(): pl.pallas_call(fit_kernel, out_shape=[jax.ShapeDtypeStruct((out_rows, COL...]
    unnamed x8 -> x4, local copies, waits for them, and re-layouts: 18.5 us -> 0.01 us
    ppermute x2 -> x3, starting transfers between devices: 4.31 us -> 16.9 us  [the longest x1 9.37 us: on_device(): theirs = lax.ppermute(mine, 'blk', other)]
  transfers between devices with their start and end apart: 5 -> 4, of which waited for: 5 -> 4; matrix products, arithmetic and copies ran while one was open for 3% -> 0% of each run, Pallas kernels for 0% -> 0%
where the time goes in v1:
time: 128 us; the launch traced here: 127 us
  blocking collectives  63.9 us (50%)
  starting transfers between devices  23.6 us (18%)
  Pallas kernels  22.5 us (18%)
  waiting for transfers between devices  13.7 us (11%)
  local copies, waits for them, and re-layouts  1.63 us (1%)
  between operations  1.43 us (1%)
    all_to_all x4, blocking collectives, swap(): return lax.all_to_all(part, 'blk', 0, 0, axis_index_groups=groups)  63.9 us
    pallas_call x1, Pallas kernels, on_device(): pl.pallas_call(fit_kernel, out_shape=[jax.ShapeDtypeStruct((out_rows, COL...  21.2 us
    ppermute x1, starting transfers between devices, on_device(): theirs = lax.ppermute(mine, 'blk', other)  9.37 us
    all_to_all x1, waiting for transfers between devices, on_device(): lax.all_to_all(jnp.broadcast_to(mine[None], (grps, share, TILE)), 'grp',...  8 us
    all_to_all x1, starting transfers between devices, on_device(): lax.all_to_all(jnp.broadcast_to(mine[None], (grps, share, TILE)), 'grp',...  6.75 us
    ppermute x1, starting transfers between devices, on_device(): tail = lax.ppermute(x[:, ROWS - TILE:], ('blk', 'grp'), following)  4.92 us
    ppermute x1, waiting for transfers between devices, on_device(): tail = lax.ppermute(x[:, ROWS - TILE:], ('blk', 'grp'), following)  3.21 us
    ppermute x1, starting transfers between devices, on_device(): mine = mine + lax.ppermute(theirs, 'blk', other)  2.6 us
  transfers between devices with their start and end apart: 4, of which 4 were waited for; matrix products, arithmetic and copies ran while one was open for 0% of the time, Pallas kernels for 0%

profile of v1, /device:TPU:1, one launch (start us, length us, event | category | flops | bytes accessed | tf_op | source)
XLA Modules:
  0.0 127.1 jit_solution(9891091805165234557)
XLA Ops:
  0.6 0.0 copy-start
  0.6 0.8 slice.4
  1.4 4.9 %collective-permute-start = (bf16[64,128]{1,0:T(8,128)(2,1)S(1)}, bf16[64,128]{1,0:T(8,128)(2,1)S(1)}, u32[]{:S(2)}, u32[]{:S(2)}) collective-permute-start(bf16[64,128]{1,0:T(8,128)(2,1)S(1)} %slice.4), channel_id=1, source_target_pairs={{0,16},{1,17},{2,18},{3,19},{4,20},{5,21},{6,22},{7,23},{8,24},{9,... | collective-permute-start | bytes 49160 | tf_op jit(solution)/shard_map/ppermute | solution.py:189
  7.0 0.0 copy-start.1
  7.0 3.2 %collective-permute-done.tail_ref = bf16[64,128]{1,0:T(8,128)(2,1)S(1)} collective-permute-done((bf16[64,128]{1,0:T(8,128)(2,1)S(1)}, bf16[64,128]{1,0:T(8,128)(2,1)S(1)}, u32[]{:S(2)}, u32[]{:S(2)}) %collective-permute-start) | collective-permute-done | bytes 16416 | tf_op jit(solution)/shard_map/ppermute | solution.py:189
  10.2 0.0 copy-done
  10.2 0.0 copy-done.1
  10.2 1.3 %shard_map.58 = (bf16[512,512]{1,0:T(8,128)(2,1)S(1)}, f32[1536,128]{1,0:T(8,128)S(1)}) custom-call(s32[1,1]{1,0:T(1,128)S(6)} %copy.6.end_ref, s32[1,512]{1,0:T(1,128)S(1)} %bitcast.22, bf16[64,128]{1,0:T(8,128)(2,1)S(1)} %collective-permute-done.tail_ref, bf16[64,512]{1,0:T(8,128)(2,1)S(1)} %bitcast.20), custom_call_target="tpu_custom_call" | custom-call | tf_op jit(solution)/shard_map/pallas_call | solution.py:190
  11.6 2.6 %collective-permute-start.1 = (f32[4,4,48,128]{3,2,1,0:T(8,128)S(1)}, f32[4,4,48,128]{3,2,1,0:T(8,128)S(1)}, u32[]{:S(2)}, u32[]{:S(2)}) collective-permute-start(f32[4,4,48,128]{3,2,1,0:T(8,128)S(1)} %dynamic-slice_bitcast_fusion), channel_id=1, source_target_pairs={{0,16},{16,0},{32,48},{48,32},{64,80},{80,64},{96,112},{112,96},{1... | collective-permute-start | bytes 1179656 | tf_op jit(solution)/shard_map/ppermute | solution.py:215
  14.2 1.3 %collective-permute-done.1 = f32[4,4,48,128]{3,2,1,0:T(8,128)S(1)} collective-permute-done((f32[4,4,48,128]{3,2,1,0:T(8,128)S(1)}, f32[4,4,48,128]{3,2,1,0:T(8,128)S(1)}, u32[]{:S(2)}, u32[]{:S(2)}) %collective-permute-start.1) | collective-permute-done | bytes 393248 | tf_op jit(solution)/shard_map/ppermute | solution.py:215
  15.6 15.1 %all_to_all.25 = f32[4,4,48,128]{3,2,1,0:T(8,128)S(1)} all-to-all(f32[4,4,48,128]{3,2,1,0:T(8,128)S(1)} %bitcast_add_fusion), channel_id=1, replica_groups={{0,32,64,96},{16,48,80,112},{128,160,192,224},{144,176,208,240},{256,28..., dimensions={0} | all-to-all | bytes 786432 | tf_op jit(solution)/shard_map/all_to_all | solution.py:209
  30.8 24.1 %all_to_all.26 = f32[4,48,128]{2,1,0:T(8,128)S(1)} all-to-all(f32[4,48,128]{2,1,0:T(8,128)S(1)} %reduce_sum.27), channel_id=1, replica_groups={{0,128,256,384},{16,144,272,400},{32,160,288,416},{48,176,304,432},{64,..., dimensions={0} | all-to-all | bytes 196608 | tf_op jit(solution)/shard_map/all_to_all | solution.py:209
  54.8 0.8 broadcast_in_dim.45
  55.6 6.8 %all-to-all-start.2 = ((f32[16,48,128]{2,1,0:T(8,128)}), f32[16,48,128]{2,1,0:T(8,128)S(1)}, u32[]{:S(2)}, u32[]{:S(2)}) async-start(f32[16,48,128]{2,1,0:T(8,128)} %broadcast_in_dim.45), calls=%async_computation.2 | async-start | bytes 786432 | tf_op jit(solution)/shard_map/all_to_all | solution.py:218
  62.4 8.0 %all-to-all-done.2 = f32[16,48,128]{2,1,0:T(8,128)S(1)} async-done(((f32[16,48,128]{2,1,0:T(8,128)}), f32[16,48,128]{2,1,0:T(8,128)S(1)}, u32[]{:S(2)}, u32[]{:S(2)}) %all-to-all-start.2) | async-done | bytes 393248 | tf_op jit(solution)/shard_map/all_to_all | solution.py:218
  70.4 0.1 select_reduce_fusion
  70.5 14.3 %all_to_all.27 = f32[4,48,128]{2,1,0:T(8,128)S(1)} all-to-all(f32[4,48,128]{2,1,0:T(8,128)S(1)} %broadcast_in_dim.47), channel_id=1, replica_groups={{0,128,256,384},{16,144,272,400},{32,160,288,416},{48,176,304,432},{64,..., dimensions={0} | all-to-all | bytes 196608 | tf_op jit(solution)/shard_map/all_to_all | solution.py:209
  84.9 10.4 %all_to_all.28 = f32[4,4,48,128]{3,2,1,0:T(8,128)S(1)} all-to-all(f32[4,4,48,128]{3,2,1,0:T(8,128)S(1)} %broadcast_in_dim.48), channel_id=1, replica_groups={{0,32,64,96},{16,48,80,112},{128,160,192,224},{144,176,208,240},{256,28..., dimensions={0} | all-to-all | bytes 786432 | tf_op jit(solution)/shard_map/all_to_all | solution.py:209
  95.3 9.4 %collective-permute-start.2 = (f32[4,4,48,128]{3,2,1,0:T(8,128)S(1)}, f32[4,4,48,128]{3,2,1,0:T(8,128)S(1)}, u32[]{:S(2)}, u32[]{:S(2)}) collective-permute-start(f32[4,4,48,128]{3,2,1,0:T(8,128)S(1)} %all_to_all.28), channel_id=1, source_target_pairs={{0,16},{16,0},{32,48},{48,32},{64,80},{80,64},{96,112},{112,96},{1... | collective-permute-start | bytes 1179656 | tf_op jit(solution)/shard_map/ppermute | solution.py:223
  104.7 1.1 collective-permute-done.2
  105.8 0.1 select_bitcast_fusion.1
  105.9 0.1 pad_maximum_fusion
  105.9 21.2 %shard_map.59 = (f32[16,512]{1,0:T(8,128)}, f32[16,64]{1,0:T(8,128)}, f32[64,512]{1,0:T(8,128)}) custom-call(s32[1,1]{1,0:T(1,128)} %bitcast.blk_ref, f32[1536,128]{1,0:T(8,128)S(1)} %bitcast.16, bf16[512,512]{1,0:T(8,128)(2,1)S(1)} %get-tuple-element.9.lagged_ref, bf16[64,512]{1,0:T(8,128)(2,1)S(1)} %bitcast.21), custom_call_target="tpu_custom_call" | custom-call | tf_op jit(solution)/shard_map/pallas_call | solution.py:229
  (7 shorter events, 0.2 us)
Async XLA Ops:
  0.6 9.6 %copy-start = (bf16[1,64,512]{2,1,0:T(8,128)(2,1)S(1)}, bf16[1,64,512]{2,1,0:T(8,128)(2,1)}, u32[]{:S(2)}) copy-start(bf16[1,64,512]{2,1,0:T(8,128)(2,1)} %param.3) | copy-start | bytes 196612
  1.4 8.8 %collective-permute-start = (bf16[64,128]{1,0:T(8,128)(2,1)S(1)}, bf16[64,128]{1,0:T(8,128)(2,1)S(1)}, u32[]{:S(2)}, u32[]{:S(2)}) collective-permute-start(bf16[64,128]{1,0:T(8,128)(2,1)S(1)} %slice.4), channel_id=1, source_target_pairs={{0,16},{1,17},{2,18},{3,19},{4,20},{5,21},{6,22},{7,23},{8,24},{9,... | collective-permute-start | bytes 49160 | tf_op jit(solution)/shard_map/ppermute | solution.py:189
  7.0 3.2 %copy-start.1 = (s32[512]{0:T(512)S(1)}, s32[512]{0:T(512)}, u32[]{:S(2)}) copy-start(s32[512]{0:T(512)} %param.4) | copy-start | bytes 6148
  11.6 3.9 %collective-permute-start.1 = (f32[4,4,48,128]{3,2,1,0:T(8,128)S(1)}, f32[4,4,48,128]{3,2,1,0:T(8,128)S(1)}, u32[]{:S(2)}, u32[]{:S(2)}) collective-permute-start(f32[4,4,48,128]{3,2,1,0:T(8,128)S(1)} %dynamic-slice_bitcast_fusion), channel_id=1, source_target_pairs={{0,16},{16,0},{32,48},{48,32},{64,80},{80,64},{96,112},{112,96},{1... | collective-permute-start | bytes 1179656 | tf_op jit(solution)/shard_map/ppermute | solution.py:215
  55.6 14.8 %all-to-all-start.2 = ((f32[16,48,128]{2,1,0:T(8,128)}), f32[16,48,128]{2,1,0:T(8,128)S(1)}, u32[]{:S(2)}, u32[]{:S(2)}) async-start(f32[16,48,128]{2,1,0:T(8,128)} %broadcast_in_dim.45), calls=%async_computation.2 | async-start | bytes 786432 | tf_op jit(solution)/shard_map/all_to_all | solution.py:218
  95.3 10.5 %collective-permute-start.2 = (f32[4,4,48,128]{3,2,1,0:T(8,128)S(1)}, f32[4,4,48,128]{3,2,1,0:T(8,128)S(1)}, u32[]{:S(2)}, u32[]{:S(2)}) collective-permute-start(f32[4,4,48,128]{3,2,1,0:T(8,128)S(1)} %all_to_all.28), channel_id=1, source_target_pairs={{0,16},{16,0},{32,48},{48,32},{64,80},{80,64},{96,112},{112,96},{1... | collective-permute-start | bytes 1179656 | tf_op jit(solution)/shard_map/ppermute | solution.py:223

commit v2 on v1

--- a/solution.py
+++ b/solution.py
@@ -198,28 +198,24 @@
         compiler_params=pltpu.CompilerParams(vmem_limit_bytes=40 << 20),
     )(window_end, lag_table[None, :], tail, x)
 
-    core, low, high = 2, 4, blks // 8
-    at = lambda h, l, c: (h * low + l) * core + c
-    near = [[at(h, l, c) for l in range(low)] for h in range(high) for c in range(core)]
-    far = [[at(h, l, c) for h in range(high)] for l in range(low) for c in range(core)]
+    core, chips = 2, blks // 2
+    column = [[z * core + c for z in range(chips)] for c in range(core)]
     other = [(i, i ^ 1) for i in range(blks)]
-    c_index = blk % 2
-
-    def swap(part, groups):
-        return lax.all_to_all(part, "blk", 0, 0, axis_index_groups=groups)
+    c_index = blk % core
+
+    def swap(part):
+        return lax.all_to_all(part, "blk", 0, 0, axis_index_groups=column)
 
     share = PACKED // blks
-    parts = packed.reshape(core, low, high, share, TILE)
+    parts = packed.reshape(core, chips, share, TILE)
     mine = lax.dynamic_index_in_dim(parts, c_index, 0, keepdims=False)
     theirs = lax.dynamic_index_in_dim(parts, 1 - c_index, 0, keepdims=False)
     mine = mine + lax.ppermute(theirs, "blk", other)
-    mine = swap(mine, near).sum(0)
-    mine = swap(mine, far).sum(0)
+    mine = swap(mine).sum(0)
     groups = lax.all_to_all(jnp.broadcast_to(mine[None], (grps, share, TILE)), "grp", 0, 0)
     until = (jnp.arange(grps) <= grp)[:, None, None]
     mine = jnp.where(until, groups, 0.0).sum(0)
-    mine = swap(jnp.broadcast_to(mine[None], (high, share, TILE)), far)
-    mine = swap(jnp.broadcast_to(mine[None], (low, high, share, TILE)), near)
+    mine = swap(jnp.broadcast_to(mine[None], (chips, share, TILE)))
     theirs = lax.ppermute(mine, "blk", other)
     first = jnp.where(c_index == 0, mine, theirs)
     second = jnp.where(c_index == 0, theirs, mine)

time: 128 us -> 124 us (0.969)
  blocking collectives: 63.9 us -> 60.1 us
    all_to_all x4 -> x2, blocking collectives: 63.9 us -> 60.1 us  [swap(): return lax.all_to_all(part, 'blk', 0, 0, axis_index_groups=column)]
where the time goes in v2:
time: 124 us
  blocking collectives  60.1 us (48%)
  starting transfers between devices  24.2 us (20%)
  Pallas kernels  22.5 us (18%)
  waiting for transfers between devices  13.6 us (11%)
  local copies, waits for them, and re-layouts  1.63 us (1%)
  between operations  1.42 us (1%)
    all_to_all x2, blocking collectives, swap(): return lax.all_to_all(part, 'blk', 0, 0, axis_index_groups=column)  60.1 us
    pallas_call x1, Pallas kernels, on_device(): pl.pallas_call(fit_kernel, out_shape=[jax.ShapeDtypeStruct((out_rows, COL...  21.2 us
    ppermute x1, starting transfers between devices, on_device(): theirs = lax.ppermute(mine, 'blk', other)  9.96 us
    all_to_all x1, waiting for transfers between devices, on_device(): lax.all_to_all(jnp.broadcast_to(mine[None], (grps, share, TILE)), 'grp',...  7.96 us
    all_to_all x1, starting transfers between devices, on_device(): lax.all_to_all(jnp.broadcast_to(mine[None], (grps, share, TILE)), 'grp',...  6.75 us
    ppermute x1, starting transfers between devices, on_device(): tail = lax.ppermute(x[:, ROWS - TILE:], ('blk', 'grp'), following)  4.92 us
    ppermute x1, waiting for transfers between devices, on_device(): tail = lax.ppermute(x[:, ROWS - TILE:], ('blk', 'grp'), following)  3.21 us
    ppermute x1, starting transfers between devices, on_device(): mine = mine + lax.ppermute(theirs, 'blk', other)  2.6 us
  transfers between devices with their start and end apart: 4, of which 4 were waited for; matrix products, arithmetic and copies ran while one was open for 0% of the time, Pallas kernels for 0%

profile of v2, /device:TPU:1, one launch (start us, length us, event | category | flops | bytes accessed | tf_op | source)
XLA Modules:
  0.0 123.9 jit_solution(11013565793296898274)
XLA Ops:
  0.6 0.0 copy-start
  0.6 0.8 slice.4
  1.4 4.9 %collective-permute-start = (bf16[64,128]{1,0:T(8,128)(2,1)S(1)}, bf16[64,128]{1,0:T(8,128)(2,1)S(1)}, u32[]{:S(2)}, u32[]{:S(2)}) collective-permute-start(bf16[64,128]{1,0:T(8,128)(2,1)S(1)} %slice.4), channel_id=1, source_target_pairs={{0,16},{1,17},{2,18},{3,19},{4,20},{5,21},{6,22},{7,23},{8,24},{9,... | collective-permute-start | bytes 49160 | tf_op jit(solution)/shard_map/ppermute | solution.py:189
  7.0 0.0 copy-start.1
  7.0 3.2 %collective-permute-done.tail_ref = bf16[64,128]{1,0:T(8,128)(2,1)S(1)} collective-permute-done((bf16[64,128]{1,0:T(8,128)(2,1)S(1)}, bf16[64,128]{1,0:T(8,128)(2,1)S(1)}, u32[]{:S(2)}, u32[]{:S(2)}) %collective-permute-start) | collective-permute-done | bytes 16416 | tf_op jit(solution)/shard_map/ppermute | solution.py:189
  10.2 0.0 copy-done
  10.2 0.0 copy-done.1
  10.2 1.3 %shard_map.58 = (bf16[512,512]{1,0:T(8,128)(2,1)S(1)}, f32[1536,128]{1,0:T(8,128)S(1)}) custom-call(s32[1,1]{1,0:T(1,128)S(6)} %copy.6.end_ref, s32[1,512]{1,0:T(1,128)S(1)} %bitcast.22, bf16[64,128]{1,0:T(8,128)(2,1)S(1)} %collective-permute-done.tail_ref, bf16[64,512]{1,0:T(8,128)(2,1)S(1)} %bitcast.20), custom_call_target="tpu_custom_call" | custom-call | tf_op jit(solution)/shard_map/pallas_call | solution.py:190
  11.6 2.6 %collective-permute-start.1 = (f32[16,48,128]{2,1,0:T(8,128)S(1)}, f32[16,48,128]{2,1,0:T(8,128)S(1)}, u32[]{:S(2)}, u32[]{:S(2)}) collective-permute-start(f32[16,48,128]{2,1,0:T(8,128)S(1)} %dynamic-slice_bitcast_fusion), channel_id=1, source_target_pairs={{0,16},{16,0},{32,48},{48,32},{64,80},{80,64},{96,112},{112,96},{1... | collective-permute-start | bytes 1179656 | tf_op jit(solution)/shard_map/ppermute | solution.py:213
  14.2 1.3 %collective-permute-done.1 = f32[16,48,128]{2,1,0:T(8,128)S(1)} collective-permute-done((f32[16,48,128]{2,1,0:T(8,128)S(1)}, f32[16,48,128]{2,1,0:T(8,128)S(1)}, u32[]{:S(2)}, u32[]{:S(2)}) %collective-permute-start.1) | collective-permute-done | bytes 393248 | tf_op jit(solution)/shard_map/ppermute | solution.py:213
  15.6 30.1 %all_to_all.15 = f32[16,48,128]{2,1,0:T(8,128)S(1)} all-to-all(f32[16,48,128]{2,1,0:T(8,128)S(1)} %bitcast_add_fusion), channel_id=1, replica_groups={{0,32,64,96,128,160,192,224,256,288,320,352,384,416,448,480},{16,48,80,..., dimensions={0} | all-to-all | bytes 786432 | tf_op jit(solution)/shard_map/all_to_all | solution.py:207
  45.8 0.8 broadcast_in_dim.39
  46.5 6.8 %all-to-all-start.1 = ((f32[16,48,128]{2,1,0:T(8,128)}), f32[16,48,128]{2,1,0:T(8,128)S(1)}, u32[]{:S(2)}, u32[]{:S(2)}) async-start(f32[16,48,128]{2,1,0:T(8,128)} %broadcast_in_dim.39), calls=%async_computation.1 | async-start | bytes 786432 | tf_op jit(solution)/shard_map/all_to_all | solution.py:215
  53.3 8.0 %all-to-all-done.1 = f32[16,48,128]{2,1,0:T(8,128)S(1)} async-done(((f32[16,48,128]{2,1,0:T(8,128)}), f32[16,48,128]{2,1,0:T(8,128)S(1)}, u32[]{:S(2)}, u32[]{:S(2)}) %all-to-all-start.1) | async-done | bytes 393248 | tf_op jit(solution)/shard_map/all_to_all | solution.py:215
  61.3 0.1 select_reduce_fusion
  61.4 30.0 %all_to_all.16 = f32[16,48,128]{2,1,0:T(8,128)S(1)} all-to-all(f32[16,48,128]{2,1,0:T(8,128)S(1)} %broadcast_in_dim.41), channel_id=1, replica_groups={{0,32,64,96,128,160,192,224,256,288,320,352,384,416,448,480},{16,48,80,..., dimensions={0} | all-to-all | bytes 786432 | tf_op jit(solution)/shard_map/all_to_all | solution.py:207
  91.4 10.0 %collective-permute-start.2 = (f32[16,48,128]{2,1,0:T(8,128)S(1)}, f32[16,48,128]{2,1,0:T(8,128)S(1)}, u32[]{:S(2)}, u32[]{:S(2)}) collective-permute-start(f32[16,48,128]{2,1,0:T(8,128)S(1)} %all_to_all.16), channel_id=1, source_target_pairs={{0,16},{16,0},{32,48},{48,32},{64,80},{80,64},{96,112},{112,96},{1... | collective-permute-start | bytes 1179656 | tf_op jit(solution)/shard_map/ppermute | solution.py:219
  101.4 1.1 collective-permute-done.2
  102.5 0.1 select_bitcast_fusion.1
  102.6 0.1 pad_maximum_fusion
  102.6 21.2 %shard_map.59 = (f32[16,512]{1,0:T(8,128)}, f32[16,64]{1,0:T(8,128)}, f32[64,512]{1,0:T(8,128)}) custom-call(s32[1,1]{1,0:T(1,128)} %bitcast.blk_ref, f32[1536,128]{1,0:T(8,128)S(1)} %bitcast.16, bf16[512,512]{1,0:T(8,128)(2,1)S(1)} %get-tuple-element.9.lagged_ref, bf16[64,512]{1,0:T(8,128)(2,1)S(1)} %bitcast.21), custom_call_target="tpu_custom_call" | custom-call | tf_op jit(solution)/shard_map/pallas_call | solution.py:225
  (5 shorter events, 0.1 us)
Async XLA Ops:
  0.6 9.6 %copy-start = (bf16[1,64,512]{2,1,0:T(8,128)(2,1)S(1)}, bf16[1,64,512]{2,1,0:T(8,128)(2,1)}, u32[]{:S(2)}) copy-start(bf16[1,64,512]{2,1,0:T(8,128)(2,1)} %param.3) | copy-start | bytes 196612
  1.4 8.8 %collective-permute-start = (bf16[64,128]{1,0:T(8,128)(2,1)S(1)}, bf16[64,128]{1,0:T(8,128)(2,1)S(1)}, u32[]{:S(2)}, u32[]{:S(2)}) collective-permute-start(bf16[64,128]{1,0:T(8,128)(2,1)S(1)} %slice.4), channel_id=1, source_target_pairs={{0,16},{1,17},{2,18},{3,19},{4,20},{5,21},{6,22},{7,23},{8,24},{9,... | collective-permute-start | bytes 49160 | tf_op jit(solution)/shard_map/ppermute | solution.py:189
  7.0 3.2 %copy-start.1 = (s32[512]{0:T(512)S(1)}, s32[512]{0:T(512)}, u32[]{:S(2)}) copy-start(s32[512]{0:T(512)} %param.4) | copy-start | bytes 6148
  11.6 3.9 %collective-permute-start.1 = (f32[16,48,128]{2,1,0:T(8,128)S(1)}, f32[16,48,128]{2,1,0:T(8,128)S(1)}, u32[]{:S(2)}, u32[]{:S(2)}) collective-permute-start(f32[16,48,128]{2,1,0:T(8,128)S(1)} %dynamic-slice_bitcast_fusion), channel_id=1, source_target_pairs={{0,16},{16,0},{32,48},{48,32},{64,80},{80,64},{96,112},{112,96},{1... | collective-permute-start | bytes 1179656 | tf_op jit(solution)/shard_map/ppermute | solution.py:213
  46.5 14.7 %all-to-all-start.1 = ((f32[16,48,128]{2,1,0:T(8,128)}), f32[16,48,128]{2,1,0:T(8,128)S(1)}, u32[]{:S(2)}, u32[]{:S(2)}) async-start(f32[16,48,128]{2,1,0:T(8,128)} %broadcast_in_dim.39), calls=%async_computation.1 | async-start | bytes 786432 | tf_op jit(solution)/shard_map/all_to_all | solution.py:215
  91.4 11.1 %collective-permute-start.2 = (f32[16,48,128]{2,1,0:T(8,128)S(1)}, f32[16,48,128]{2,1,0:T(8,128)S(1)}, u32[]{:S(2)}, u32[]{:S(2)}) collective-permute-start(f32[16,48,128]{2,1,0:T(8,128)S(1)} %all_to_all.16), channel_id=1, source_target_pairs={{0,16},{16,0},{32,48},{48,32},{64,80},{80,64},{96,112},{112,96},{1... | collective-permute-start | bytes 1179656 | tf_op jit(solution)/shard_map/ppermute | solution.py:219

commit v3 on v2

--- a/solution.py
+++ b/solution.py
@@ -55,7 +55,7 @@
     packed_ref[n * TILE :, :] = jnp.concatenate([cross[:half], cross[half:]], axis=1)
 
 
-def factor_tile(d_rows):
+def factor_tile(d_rows, rows_ref):
     n = len(d_rows)
     lane = lax.broadcasted_iota(jnp.int32, (8, TILE), 1)
     sub = lax.broadcasted_iota(jnp.int32, (8, TILE), 0)
@@ -65,55 +65,58 @@
     def col(v, c):
         return jnp.broadcast_to(v[:, c : c + 1], (8, TILE))
 
-    def row(v, i):
-        return jnp.broadcast_to(v[i : i + 1, :], (8, TILE))
+    def less(v, a, b):
+        t = [a[i] * b[i] for i in range(8)]
+        return v - (((t[0] + t[1]) + (t[2] + t[3])) + ((t[4] + t[5]) + (t[6] + t[7])))
 
     for p in range(n):
         base = 8 * p
-        c = [col(d[p], base + j) for j in range(8)]
-        s = {(i, j): row(c[j], i) for j in range(8) for i in range(j + 1)}
-        r = [row(d[p], i) for i in range(8)]
-        xr = [row(x[p], i) for i in range(8)]
+
+        def rows_of(v, slot, count):
+            at = 8 * (slot + 10 * (p % 2))
+            rows_ref[at : at + 8, :] = v
+            return [jnp.broadcast_to(rows_ref[at + i : at + i + 1, :], (8, TILE)) for i in range(count)]
+
+        s = {}
+        for j in range(8):
+            for i, v in enumerate(rows_of(col(d[p], base + j), j, j + 1)):
+                s[i, j] = v
+        r = rows_of(d[p], 8, 8)
+        xr = rows_of(x[p], 9, 8)
         cn = [col(d[p + 1], base + j) for j in range(8)] if p + 1 < n else []
-        u = {}
-        inv = []
-        for k in range(8):
-            w = lax.rsqrt(s[k, k])
-            inv.append(w)
-            for j in range(k + 1, 8):
-                u[k, j] = s[k, j] * w
-            for i in range(k + 1, 8):
+        sets = [v for v in (r, xr, cn) if v]
+        u, inv = {}, [None] * 8
+        for k in range(0, 8, 2):
+            one, off, two = s[k, k], s[k, k + 1], s[k + 1, k + 1]
+            w0 = lax.rsqrt(one)
+            w1 = lax.rsqrt((one * two - off * off) * one) * one
+            inv[k], inv[k + 1] = w0, w1
+            u[k, k + 1] = off * w0
+            for j in range(k + 2, 8):
+                u[k, j] = s[k, j] * w0
+                u[k + 1, j] = (s[k + 1, j] - u[k, k + 1] * u[k, j]) * w1
+            for i in range(k + 2, 8):
                 for j in range(i, 8):
-                    s[i, j] = s[i, j] - u[k, i] * u[k, j]
-            r[k] = r[k] * w
-            xr[k] = xr[k] * w
-            if cn:
-                cn[k] = cn[k] * w
-            for i in range(k + 1, 8):
-                r[i] = r[i] - u[k, i] * r[k]
-                xr[i] = xr[i] - u[k, i] * xr[k]
-                if cn:
-                    cn[i] = cn[i] - u[k, i] * cn[k]
+                    s[i, j] = (s[i, j] - u[k, i] * u[k, j]) - u[k + 1, i] * u[k + 1, j]
+            for v in sets:
+                v[k] = v[k] * w0
+                v[k + 1] = (v[k + 1] - u[k, k + 1] * v[k]) * w1
+                for i in range(k + 2, 8):
+                    v[i] = (v[i] - u[k, i] * v[k]) - u[k + 1, i] * v[k + 1]
         if p + 1 < n:
-            t = [cn[i] * r[i] for i in range(8)]
-            d[p + 1] = d[p + 1] - (((t[0] + t[1]) + (t[2] + t[3])) + ((t[4] + t[5]) + (t[6] + t[7])))
-            t = [cn[i] * xr[i] for i in range(8)]
-            x[p + 1] = x[p + 1] - (((t[0] + t[1]) + (t[2] + t[3])) + ((t[4] + t[5]) + (t[6] + t[7])))
+            d[p + 1] = less(d[p + 1], cn, r)
+            x[p + 1] = less(x[p + 1], cn, xr)
         if p + 2 < n:
-            z = list(r)
-            xz = list(xr)
+            z, xz = list(r), list(xr)
             for k in reversed(range(8)):
-                z[k] = z[k] * inv[k]
-                xz[k] = xz[k] * inv[k]
-                for i in range(k):
-                    z[i] = z[i] - u[i, k] * z[k]
-                    xz[i] = xz[i] - u[i, k] * xz[k]
+                for v in (z, xz):
+                    v[k] = v[k] * inv[k]
+                    for i in range(k):
+                        v[i] = v[i] - u[i, k] * v[k]
             for q in range(p + 2, n):
                 cq = [col(d[q], base + j) for j in range(8)]
-                t = [cq[i] * z[i] for i in range(8)]
-                d[q] = d[q] - (((t[0] + t[1]) + (t[2] + t[3])) + ((t[4] + t[5]) + (t[6] + t[7])))
-                t = [cq[i] * xz[i] for i in range(8)]
-                x[q] = x[q] - (((t[0] + t[1]) + (t[2] + t[3])) + ((t[4] + t[5]) + (t[6] + t[7])))
+                d[q] = less(d[q], cq, z)
+                x[q] = less(x[q], cq, xz)
         du, dx = r[0], xr[0]
         for i in range(1, 8):
             du = jnp.where(sub == i, r[i], du)
@@ -123,7 +126,7 @@
     return d, x
 
 
-def fit_kernel(blk_ref, packed_ref, lagged_ref, x_ref, factor_ref, coef_ref, resid_ref, u_ref, i_ref, w_ref):
+def fit_kernel(blk_ref, packed_ref, lagged_ref, x_ref, factor_ref, coef_ref, resid_ref, u_ref, w_ref, rows_ref):
     high = lax.Precision.HIGHEST
     half = COLS // 2
     tiles = {}
@@ -138,29 +141,32 @@
         b.append(packed_ref[at : at + TILE, lo : lo + SENSORS])
     u_ref[...] = jnp.zeros_like(u_ref)
     y = []
-    for k in range(NT):
-        d, xi = factor_tile([g[k, k][8 * q : 8 * q + 8] for q in range(TILE // 8)])
+    e = {}
+    for k in range(NT):
+        d, xi = factor_tile([g[k, k][8 * q : 8 * q + 8] for q in range(TILE // 8)], rows_ref)
         ukk = jnp.concatenate(d, axis=0)
         xkk = jnp.concatenate(xi, axis=0)
-        i_ref[k * TILE : (k + 1) * TILE, :] = xkk
         u_ref[k * TILE : (k + 1) * TILE, k * TILE : (k + 1) * TILE] = ukk
         panel = {}
         for j in range(k + 1, NT):
             panel[j] = dot(xkk, g[k, j], 1, 0, high)
             u_ref[k * TILE : (k + 1) * TILE, j * TILE : (j + 1) * TILE] = panel[j]
         y.append(dot(xkk, b[k], 1, 0, high))
+        e[k, k] = xkk
+        for i in range(k):
+            e[k, i] = dot(xkk, e[k, i], 1, 0, high)
         for i in range(k + 1, NT):
             for j in range(i, NT):
                 g[i, j] = g[i, j] - dot(panel[i], panel[j], 0, 0, high)
             b[i] = b[i] - dot(panel[i], y[k], 0, 0, high)
-    w = [None] * NT
-    for k in reversed(range(NT)):
-        acc = y[k]
+            for h in range(k + 1):
+                past = dot(panel[i], e[k, h], 0, 0, high)
+                e[i, h] = e[i, h] - past if (i, h) in e else -past
+    for k in range(NT):
+        acc = dot(e[k, k], y[k], 0, 0, high)
         for j in range(k + 1, NT):
-            ukj = u_ref[k * TILE : (k + 1) * TILE, j * TILE : (j + 1) * TILE]
-            acc = acc - dot(ukj, w[j], 1, 0, high)
-        w[k] = dot(i_ref[k * TILE : (k + 1) * TILE, :], acc, 0, 0, high)
-        w_ref[k * TILE : (k + 1) * TILE, :] = w[k]
+            acc = acc + dot(e[j, k], y[j], 0, 0, high)
+        w_ref[k * TILE : (k + 1) * TILE, :] = acc
     share = factor_ref.shape[0]
     first = pl.multiple_of(blk_ref[0, 0] * share, 8)
     factor_ref[...] = u_ref[pl.ds(first, share), :] * (1.0 / 128.0)
@@ -233,8 +239,8 @@
         out_specs=[VMEM, VMEM, VMEM],
         scratch_shapes=[
             pltpu.VMEM((COLS, COLS), F32),
-            pltpu.VMEM((COLS, TILE), F32),
             pltpu.VMEM((COLS, SENSORS), F32),
+            pltpu.VMEM((160, TILE), F32),
         ],
         compiler_params=pltpu.CompilerParams(vmem_limit_bytes=40 << 20),
     )(blk.reshape(1, 1), prefix, lagged, x)

time: 124 us -> 118 us (0.952)
  Pallas kernels: 22.5 us -> 16.7 us
    pallas_call x1, Pallas kernels: 21.2 us -> 15.4 us  [on_device(): pl.pallas_call(fit_kernel, out_shape=[jax.ShapeDtypeStruct((out_rows, COL...]
where the time goes in v3:
time: 118 us
  blocking collectives  60.1 us (51%)
  starting transfers between devices  24.2 us (21%)
  Pallas kernels  16.7 us (14%)
  waiting for transfers between devices  13.6 us (12%)
  local copies, waits for them, and re-layouts  1.63 us (1%)
  between operations  1.42 us (1%)
    all_to_all x2, blocking collectives, swap(): return lax.all_to_all(part, 'blk', 0, 0, axis_index_groups=column)  60.1 us
    pallas_call x1, Pallas kernels, on_device(): pl.pallas_call(fit_kernel, out_shape=[jax.ShapeDtypeStruct((out_rows, COL...  15.4 us
    ppermute x1, starting transfers between devices, on_device(): theirs = lax.ppermute(mine, 'blk', other)  9.96 us
    all_to_all x1, waiting for transfers between devices, on_device(): lax.all_to_all(jnp.broadcast_to(mine[None], (grps, share, TILE)), 'grp',...  7.96 us
    all_to_all x1, starting transfers between devices, on_device(): lax.all_to_all(jnp.broadcast_to(mine[None], (grps, share, TILE)), 'grp',...  6.75 us
    ppermute x1, starting transfers between devices, on_device(): tail = lax.ppermute(x[:, ROWS - TILE:], ('blk', 'grp'), following)  4.92 us
    ppermute x1, waiting for transfers between devices, on_device(): tail = lax.ppermute(x[:, ROWS - TILE:], ('blk', 'grp'), following)  3.21 us
    ppermute x1, starting transfers between devices, on_device(): mine = mine + lax.ppermute(theirs, 'blk', other)  2.6 us
  transfers between devices with their start and end apart: 4, of which 4 were waited for; matrix products, arithmetic and copies ran while one was open for 0% of the time, Pallas kernels for 0%

profile of v3, /device:TPU:1, one launch (start us, length us, event | category | flops | bytes accessed | tf_op | source)
XLA Modules:
  0.0 118.0 jit_solution(12224678614965453635)
XLA Ops:
  0.6 0.0 copy-start
  0.6 0.8 slice.4
  1.4 4.9 %collective-permute-start = (bf16[64,128]{1,0:T(8,128)(2,1)S(1)}, bf16[64,128]{1,0:T(8,128)(2,1)S(1)}, u32[]{:S(2)}, u32[]{:S(2)}) collective-permute-start(bf16[64,128]{1,0:T(8,128)(2,1)S(1)} %slice.4), channel_id=1, source_target_pairs={{0,16},{1,17},{2,18},{3,19},{4,20},{5,21},{6,22},{7,23},{8,24},{9,... | collective-permute-start | bytes 49160 | tf_op jit(solution)/shard_map/ppermute | solution.py:195
  7.0 0.0 copy-start.1
  7.0 3.2 %collective-permute-done.tail_ref = bf16[64,128]{1,0:T(8,128)(2,1)S(1)} collective-permute-done((bf16[64,128]{1,0:T(8,128)(2,1)S(1)}, bf16[64,128]{1,0:T(8,128)(2,1)S(1)}, u32[]{:S(2)}, u32[]{:S(2)}) %collective-permute-start) | collective-permute-done | bytes 16416 | tf_op jit(solution)/shard_map/ppermute | solution.py:195
  10.2 0.0 copy-done
  10.2 0.0 copy-done.1
  10.2 1.3 %shard_map.58 = (bf16[512,512]{1,0:T(8,128)(2,1)S(1)}, f32[1536,128]{1,0:T(8,128)S(1)}) custom-call(s32[1,1]{1,0:T(1,128)S(6)} %copy.6.end_ref, s32[1,512]{1,0:T(1,128)S(1)} %bitcast.22, bf16[64,128]{1,0:T(8,128)(2,1)S(1)} %collective-permute-done.tail_ref, bf16[64,512]{1,0:T(8,128)(2,1)S(1)} %bitcast.20), custom_call_target="tpu_custom_call" | custom-call | tf_op jit(solution)/shard_map/pallas_call | solution.py:196
  11.6 2.6 %collective-permute-start.1 = (f32[16,48,128]{2,1,0:T(8,128)S(1)}, f32[16,48,128]{2,1,0:T(8,128)S(1)}, u32[]{:S(2)}, u32[]{:S(2)}) collective-permute-start(f32[16,48,128]{2,1,0:T(8,128)S(1)} %dynamic-slice_bitcast_fusion), channel_id=1, source_target_pairs={{0,16},{16,0},{32,48},{48,32},{64,80},{80,64},{96,112},{112,96},{1... | collective-permute-start | bytes 1179656 | tf_op jit(solution)/shard_map/ppermute | solution.py:219
  14.2 1.3 %collective-permute-done.1 = f32[16,48,128]{2,1,0:T(8,128)S(1)} collective-permute-done((f32[16,48,128]{2,1,0:T(8,128)S(1)}, f32[16,48,128]{2,1,0:T(8,128)S(1)}, u32[]{:S(2)}, u32[]{:S(2)}) %collective-permute-start.1) | collective-permute-done | bytes 393248 | tf_op jit(solution)/shard_map/ppermute | solution.py:219
  15.6 30.1 %all_to_all.15 = f32[16,48,128]{2,1,0:T(8,128)S(1)} all-to-all(f32[16,48,128]{2,1,0:T(8,128)S(1)} %bitcast_add_fusion), channel_id=1, replica_groups={{0,32,64,96,128,160,192,224,256,288,320,352,384,416,448,480},{16,48,80,..., dimensions={0} | all-to-all | bytes 786432 | tf_op jit(solution)/shard_map/all_to_all | solution.py:213
  45.8 0.8 broadcast_in_dim.39
  46.5 6.8 %all-to-all-start.1 = ((f32[16,48,128]{2,1,0:T(8,128)}), f32[16,48,128]{2,1,0:T(8,128)S(1)}, u32[]{:S(2)}, u32[]{:S(2)}) async-start(f32[16,48,128]{2,1,0:T(8,128)} %broadcast_in_dim.39), calls=%async_computation.1 | async-start | bytes 786432 | tf_op jit(solution)/shard_map/all_to_all | solution.py:221
  53.3 8.0 %all-to-all-done.1 = f32[16,48,128]{2,1,0:T(8,128)S(1)} async-done(((f32[16,48,128]{2,1,0:T(8,128)}), f32[16,48,128]{2,1,0:T(8,128)S(1)}, u32[]{:S(2)}, u32[]{:S(2)}) %all-to-all-start.1) | async-done | bytes 393248 | tf_op jit(solution)/shard_map/all_to_all | solution.py:221
  61.3 0.1 select_reduce_fusion
  61.4 30.0 %all_to_all.16 = f32[16,48,128]{2,1,0:T(8,128)S(1)} all-to-all(f32[16,48,128]{2,1,0:T(8,128)S(1)} %broadcast_in_dim.41), channel_id=1, replica_groups={{0,32,64,96,128,160,192,224,256,288,320,352,384,416,448,480},{16,48,80,..., dimensions={0} | all-to-all | bytes 786432 | tf_op jit(solution)/shard_map/all_to_all | solution.py:213
  91.4 10.0 %collective-permute-start.2 = (f32[16,48,128]{2,1,0:T(8,128)S(1)}, f32[16,48,128]{2,1,0:T(8,128)S(1)}, u32[]{:S(2)}, u32[]{:S(2)}) collective-permute-start(f32[16,48,128]{2,1,0:T(8,128)S(1)} %all_to_all.16), channel_id=1, source_target_pairs={{0,16},{16,0},{32,48},{48,32},{64,80},{80,64},{96,112},{112,96},{1... | collective-permute-start | bytes 1179656 | tf_op jit(solution)/shard_map/ppermute | solution.py:225
  101.4 1.1 collective-permute-done.2
  102.5 0.1 select_bitcast_fusion.1
  102.6 0.1 pad_maximum_fusion
  102.6 15.4 %shard_map.59 = (f32[16,512]{1,0:T(8,128)}, f32[16,64]{1,0:T(8,128)}, f32[64,512]{1,0:T(8,128)}) custom-call(s32[1,1]{1,0:T(1,128)} %bitcast.blk_ref, f32[1536,128]{1,0:T(8,128)S(1)} %bitcast.16, bf16[512,512]{1,0:T(8,128)(2,1)S(1)} %get-tuple-element.9.lagged_ref, bf16[64,512]{1,0:T(8,128)(2,1)S(1)} %bitcast.21), custom_call_target="tpu_custom_call" | custom-call | tf_op jit(solution)/shard_map/pallas_call | solution.py:231
  (5 shorter events, 0.1 us)
Async XLA Ops:
  0.6 9.6 %copy-start = (bf16[1,64,512]{2,1,0:T(8,128)(2,1)S(1)}, bf16[1,64,512]{2,1,0:T(8,128)(2,1)}, u32[]{:S(2)}) copy-start(bf16[1,64,512]{2,1,0:T(8,128)(2,1)} %param.3) | copy-start | bytes 196612
  1.4 8.8 %collective-permute-start = (bf16[64,128]{1,0:T(8,128)(2,1)S(1)}, bf16[64,128]{1,0:T(8,128)(2,1)S(1)}, u32[]{:S(2)}, u32[]{:S(2)}) collective-permute-start(bf16[64,128]{1,0:T(8,128)(2,1)S(1)} %slice.4), channel_id=1, source_target_pairs={{0,16},{1,17},{2,18},{3,19},{4,20},{5,21},{6,22},{7,23},{8,24},{9,... | collective-permute-start | bytes 49160 | tf_op jit(solution)/shard_map/ppermute | solution.py:195
  7.0 3.2 %copy-start.1 = (s32[512]{0:T(512)S(1)}, s32[512]{0:T(512)}, u32[]{:S(2)}) copy-start(s32[512]{0:T(512)} %param.4) | copy-start | bytes 6148
  11.6 3.9 %collective-permute-start.1 = (f32[16,48,128]{2,1,0:T(8,128)S(1)}, f32[16,48,128]{2,1,0:T(8,128)S(1)}, u32[]{:S(2)}, u32[]{:S(2)}) collective-permute-start(f32[16,48,128]{2,1,0:T(8,128)S(1)} %dynamic-slice_bitcast_fusion), channel_id=1, source_target_pairs={{0,16},{16,0},{32,48},{48,32},{64,80},{80,64},{96,112},{112,96},{1... | collective-permute-start | bytes 1179656 | tf_op jit(solution)/shard_map/ppermute | solution.py:219
  46.5 14.7 %all-to-all-start.1 = ((f32[16,48,128]{2,1,0:T(8,128)}), f32[16,48,128]{2,1,0:T(8,128)S(1)}, u32[]{:S(2)}, u32[]{:S(2)}) async-start(f32[16,48,128]{2,1,0:T(8,128)} %broadcast_in_dim.39), calls=%async_computation.1 | async-start | bytes 786432 | tf_op jit(solution)/shard_map/all_to_all | solution.py:221
  91.4 11.1 %collective-permute-start.2 = (f32[16,48,128]{2,1,0:T(8,128)S(1)}, f32[16,48,128]{2,1,0:T(8,128)S(1)}, u32[]{:S(2)}, u32[]{:S(2)}) collective-permute-start(f32[16,48,128]{2,1,0:T(8,128)S(1)} %all_to_all.16), channel_id=1, source_target_pairs={{0,16},{16,0},{32,48},{48,32},{64,80},{80,64},{96,112},{112,96},{1... | collective-permute-start | bytes 1179656 | tf_op jit(solution)/shard_map/ppermute | solution.py:225

commit v4 on v3

--- a/solution.py
+++ b/solution.py
@@ -213,19 +213,15 @@
         return lax.all_to_all(part, "blk", 0, 0, axis_index_groups=column)
 
     share = PACKED // blks
-    parts = packed.reshape(core, chips, share, TILE)
-    mine = lax.dynamic_index_in_dim(parts, c_index, 0, keepdims=False)
-    theirs = lax.dynamic_index_in_dim(parts, 1 - c_index, 0, keepdims=False)
+    parts = packed.reshape(chips, core, share, TILE)
+    mine = lax.dynamic_index_in_dim(parts, c_index, 1, keepdims=False)
+    theirs = lax.dynamic_index_in_dim(parts, 1 - c_index, 1, keepdims=False)
     mine = mine + lax.ppermute(theirs, "blk", other)
     mine = swap(mine).sum(0)
     groups = lax.all_to_all(jnp.broadcast_to(mine[None], (grps, share, TILE)), "grp", 0, 0)
     until = (jnp.arange(grps) <= grp)[:, None, None]
     mine = jnp.where(until, groups, 0.0).sum(0)
-    mine = swap(jnp.broadcast_to(mine[None], (chips, share, TILE)))
-    theirs = lax.ppermute(mine, "blk", other)
-    first = jnp.where(c_index == 0, mine, theirs)
-    second = jnp.where(c_index == 0, theirs, mine)
-    prefix = jnp.stack([first, second]).reshape(PACKED, TILE)
+    prefix = lax.all_gather(mine, "blk", axis=0, tiled=True)
 
     out_rows = COLS // blks
     factor, coef, resid = pl.pallas_call(

time: 118 us -> 119 us (level)
  blocking collectives: 60.1 us -> 71.8 us
  starting transfers between devices: 24.2 us -> 14.3 us
    all_gather x0 -> x1, blocking collectives: none -> 41.7 us  [on_device(): prefix = lax.all_gather(mine, 'blk', axis=0, tiled=True)]
    all_to_all x2 -> x1, blocking collectives: 60.1 us -> 30.2 us  [swap(): return lax.all_to_all(part, 'blk', 0, 0, axis_index_groups=column)]
    ppermute x1 -> x0, starting transfers between devices: 9.96 us -> none  [on_device(): theirs = lax.ppermute(mine, 'blk', other)]
  transfers between devices with their start and end apart: 4 -> 3, of which waited for: 4 -> 3; matrix products, arithmetic and copies ran while one was open for 0% -> 0% of each run, Pallas kernels for 0% -> 0%
where the time goes in v4:
time: 119 us; the launch traced here: 118 us
  blocking collectives  71.8 us (60%)
  Pallas kernels  16.7 us (14%)
  starting transfers between devices  14.3 us (12%)
  waiting for transfers between devices  12.5 us (11%)
  local copies, waits for them, and re-layouts  1.61 us (1%)
  between operations  1.38 us (1%)
    all_gather x1, blocking collectives, on_device(): prefix = lax.all_gather(mine, 'blk', axis=0, tiled=True)  41.7 us
    all_to_all x1, blocking collectives, swap(): return lax.all_to_all(part, 'blk', 0, 0, axis_index_groups=column)  30.2 us
    pallas_call x1, Pallas kernels, on_device(): pl.pallas_call(fit_kernel, out_shape=[jax.ShapeDtypeStruct((out_rows, COL...  15.4 us
    all_to_all x1, waiting for transfers between devices, on_device(): lax.all_to_all(jnp.broadcast_to(mine[None], (grps, share, TILE)), 'grp',...  7.96 us
    all_to_all x1, starting transfers between devices, on_device(): lax.all_to_all(jnp.broadcast_to(mine[None], (grps, share, TILE)), 'grp',...  6.76 us
    ppermute x1, starting transfers between devices, on_device(): tail = lax.ppermute(x[:, ROWS - TILE:], ('blk', 'grp'), following)  4.92 us
    ppermute x1, waiting for transfers between devices, on_device(): tail = lax.ppermute(x[:, ROWS - TILE:], ('blk', 'grp'), following)  3.21 us
    ppermute x1, starting transfers between devices, on_device(): mine = mine + lax.ppermute(theirs, 'blk', other)  2.59 us
  transfers between devices with their start and end apart: 3, of which 3 were waited for; matrix products, arithmetic and copies ran while one was open for 0% of the time, Pallas kernels for 0%

profile of v4, /device:TPU:1, one launch (start us, length us, event | category | flops | bytes accessed | tf_op | source)
XLA Modules:
  0.0 118.5 jit_solution(436655678096993390)
XLA Ops:
  0.6 0.0 copy-start
  0.6 0.8 slice.4
  1.4 4.9 %collective-permute-start = (bf16[64,128]{1,0:T(8,128)(2,1)S(1)}, bf16[64,128]{1,0:T(8,128)(2,1)S(1)}, u32[]{:S(2)}, u32[]{:S(2)}) collective-permute-start(bf16[64,128]{1,0:T(8,128)(2,1)S(1)} %slice.4), channel_id=1, source_target_pairs={{0,16},{1,17},{2,18},{3,19},{4,20},{5,21},{6,22},{7,23},{8,24},{9,... | collective-permute-start | bytes 49160 | tf_op jit(solution)/shard_map/ppermute | solution.py:195
  7.0 0.0 copy-start.1
  7.0 3.2 %collective-permute-done.tail_ref = bf16[64,128]{1,0:T(8,128)(2,1)S(1)} collective-permute-done((bf16[64,128]{1,0:T(8,128)(2,1)S(1)}, bf16[64,128]{1,0:T(8,128)(2,1)S(1)}, u32[]{:S(2)}, u32[]{:S(2)}) %collective-permute-start) | collective-permute-done | bytes 16416 | tf_op jit(solution)/shard_map/ppermute | solution.py:195
  10.2 0.0 copy-done
  10.2 0.0 copy-done.1
  10.2 1.3 %shard_map.58 = (bf16[512,512]{1,0:T(8,128)(2,1)S(1)}, f32[1536,128]{1,0:T(8,128)S(1)}) custom-call(s32[1,1]{1,0:T(1,128)S(6)} %copy.6.end_ref, s32[1,512]{1,0:T(1,128)S(1)} %bitcast.16, bf16[64,128]{1,0:T(8,128)(2,1)S(1)} %collective-permute-done.tail_ref, bf16[64,512]{1,0:T(8,128)(2,1)S(1)} %bitcast.14), custom_call_target="tpu_custom_call" | custom-call | tf_op jit(solution)/shard_map/pallas_call | solution.py:196
  11.6 2.6 %collective-permute-start.1 = (f32[16,48,128]{2,1,0:T(8,128)S(1)}, f32[16,48,128]{2,1,0:T(8,128)S(1)}, u32[]{:S(2)}, u32[]{:S(2)}) collective-permute-start(f32[16,48,128]{2,1,0:T(8,128)S(1)} %dynamic-slice_bitcast_fusion), channel_id=1, source_target_pairs={{0,16},{16,0},{32,48},{48,32},{64,80},{80,64},{96,112},{112,96},{1... | collective-permute-start | bytes 1179656 | tf_op jit(solution)/shard_map/ppermute | solution.py:219
  14.2 1.3 %collective-permute-done.1 = f32[16,48,128]{2,1,0:T(8,128)S(1)} collective-permute-done((f32[16,48,128]{2,1,0:T(8,128)S(1)}, f32[16,48,128]{2,1,0:T(8,128)S(1)}, u32[]{:S(2)}, u32[]{:S(2)}) %collective-permute-start.1) | collective-permute-done | bytes 393248 | tf_op jit(solution)/shard_map/ppermute | solution.py:219
  15.6 0.1 bitcast_add_fusion
  15.6 30.2 %all_to_all.10 = f32[16,48,128]{2,1,0:T(8,128)S(1)} all-to-all(f32[16,48,128]{2,1,0:T(8,128)S(1)} %bitcast_add_fusion), channel_id=1, replica_groups={{0,32,64,96,128,160,192,224,256,288,320,352,384,416,448,480},{16,48,80,..., dimensions={0} | all-to-all | bytes 786432 | tf_op jit(solution)/shard_map/all_to_all | solution.py:213
  45.8 0.8 broadcast_in_dim.33
  46.6 6.8 %all-to-all-start.1 = ((f32[16,48,128]{2,1,0:T(8,128)}), f32[16,48,128]{2,1,0:T(8,128)S(1)}, u32[]{:S(2)}, u32[]{:S(2)}) async-start(f32[16,48,128]{2,1,0:T(8,128)} %broadcast_in_dim.33), calls=%async_computation.1 | async-start | bytes 786432 | tf_op jit(solution)/shard_map/all_to_all | solution.py:221
  53.4 8.0 %all-to-all-done.1 = f32[16,48,128]{2,1,0:T(8,128)S(1)} async-done(((f32[16,48,128]{2,1,0:T(8,128)}), f32[16,48,128]{2,1,0:T(8,128)S(1)}, u32[]{:S(2)}, u32[]{:S(2)}) %all-to-all-start.1) | async-done | bytes 393248 | tf_op jit(solution)/shard_map/all_to_all | solution.py:221
  61.3 0.1 select_reduce_fusion
  61.4 41.7 %all_gather.3.packed_ref = f32[1536,128]{1,0:T(8,128)S(1)} all-gather(f32[48,128]{1,0:T(8,128)S(1)} %select_reduce_fusion), channel_id=1, replica_groups=mesh['blk'=32,'grp'=16] {'blk'}, dimensions={0}, use_global_device_ids=true | all-gather | bytes 811008 | tf_op jit(solution)/shard_map/all_gather | solution.py:224
  103.1 15.4 %shard_map.59 = (f32[16,512]{1,0:T(8,128)}, f32[16,64]{1,0:T(8,128)}, f32[64,512]{1,0:T(8,128)}) custom-call(s32[1,1]{1,0:T(1,128)} %bitcast.blk_ref, f32[1536,128]{1,0:T(8,128)S(1)} %all_gather.3.packed_ref, bf16[512,512]{1,0:T(8,128)(2,1)S(1)} %get-tuple-element.9.lagged_ref, bf16[64,512]{1,0:T(8,128)(2,1)S(1)} %bitcast.15), custom_call_target="tpu_custom_call" | custom-call | tf_op jit(solution)/shard_map/pallas_call | solution.py:227
  (3 shorter events, 0.1 us)
Async XLA Ops:
  0.6 9.6 %copy-start = (bf16[1,64,512]{2,1,0:T(8,128)(2,1)S(1)}, bf16[1,64,512]{2,1,0:T(8,128)(2,1)}, u32[]{:S(2)}) copy-start(bf16[1,64,512]{2,1,0:T(8,128)(2,1)} %param.3) | copy-start | bytes 196612
  1.4 8.8 %collective-permute-start = (bf16[64,128]{1,0:T(8,128)(2,1)S(1)}, bf16[64,128]{1,0:T(8,128)(2,1)S(1)}, u32[]{:S(2)}, u32[]{:S(2)}) collective-permute-start(bf16[64,128]{1,0:T(8,128)(2,1)S(1)} %slice.4), channel_id=1, source_target_pairs={{0,16},{1,17},{2,18},{3,19},{4,20},{5,21},{6,22},{7,23},{8,24},{9,... | collective-permute-start | bytes 49160 | tf_op jit(solution)/shard_map/ppermute | solution.py:195
  7.0 3.2 %copy-start.1 = (s32[512]{0:T(512)S(1)}, s32[512]{0:T(512)}, u32[]{:S(2)}) copy-start(s32[512]{0:T(512)} %param.4) | copy-start | bytes 6148
  11.6 3.9 %collective-permute-start.1 = (f32[16,48,128]{2,1,0:T(8,128)S(1)}, f32[16,48,128]{2,1,0:T(8,128)S(1)}, u32[]{:S(2)}, u32[]{:S(2)}) collective-permute-start(f32[16,48,128]{2,1,0:T(8,128)S(1)} %dynamic-slice_bitcast_fusion), channel_id=1, source_target_pairs={{0,16},{16,0},{32,48},{48,32},{64,80},{80,64},{96,112},{112,96},{1... | collective-permute-start | bytes 1179656 | tf_op jit(solution)/shard_map/ppermute | solution.py:219
  46.6 14.7 %all-to-all-start.1 = ((f32[16,48,128]{2,1,0:T(8,128)}), f32[16,48,128]{2,1,0:T(8,128)S(1)}, u32[]{:S(2)}, u32[]{:S(2)}) async-start(f32[16,48,128]{2,1,0:T(8,128)} %broadcast_in_dim.33), calls=%async_computation.1 | async-start | bytes 786432 | tf_op jit(solution)/shard_map/all_to_all | solution.py:221

commit v5 on v4

--- a/solution.py
+++ b/solution.py
@@ -14,8 +14,9 @@
 ROWS = 512
 TILE = 128
 NT = COLS // TILE
-TILES = [(k, j) for k in range(NT) for j in range(k, NT)]
-PACKED = (len(TILES) + NT // 2) * TILE
+TILES = [(k, j) for k in range(NT) for j in range(k + 1, NT)]
+PACKED = (len(TILES) + NT // 2 + NT // 2) * TILE
+SPARE = 8
 VMEM = pl.BlockSpec(memory_space=pltpu.VMEM)
 SMEM = pl.BlockSpec(memory_space=pltpu.SMEM)
 
@@ -26,7 +27,7 @@
     )
 
 
-def gram_kernel(end_ref, table_ref, tail_ref, x_ref, lagged_ref, packed_ref):
+def gram_kernel(end_ref, table_ref, tail_ref, x_ref, lagged_ref, packed_ref, spare_ref):
     x = x_ref[...]
     ext = jnp.concatenate([tail_ref[...], x], axis=1).astype(F32)
     pieces = [pltpu.roll(ext, d, 1)[:, TILE:].astype(BF16) for d in range(1, LAGS + 1)]
@@ -37,22 +38,28 @@
     lagged_ref[...] = lagged
     time = lax.broadcasted_iota(jnp.int32, (COLS, ROWS), 1)
     masked = jnp.where(time < end_ref[0, 0], lagged.astype(F32), 0.0).astype(BF16)
-    eye = (
-        lax.broadcasted_iota(jnp.int32, (TILE, TILE), 0)
-        == lax.broadcasted_iota(jnp.int32, (TILE, TILE), 1)
-    )
-    ridge = jnp.where(eye, RIDGE, 0.0)
-    n = 0
+    row = lax.broadcasted_iota(jnp.int32, (TILE, TILE), 0)
+    column = lax.broadcasted_iota(jnp.int32, (TILE, TILE), 1)
+    spare_ref[...] = jnp.zeros_like(spare_ref)
     for k in range(NT):
         rows = masked[k * TILE : (k + 1) * TILE]
         block = dot(rows, lagged[k * TILE :], 1, 1)
-        for j in range(k, NT):
-            tile = block[:, (j - k) * TILE : (j - k + 1) * TILE]
-            packed_ref[n * TILE : (n + 1) * TILE, :] = tile + ridge if j == k else tile
-            n += 1
+        for j in range(k + 1, NT):
+            n = TILES.index((k, j)) * TILE
+            packed_ref[n : n + TILE, :] = block[:, (j - k) * TILE : (j - k + 1) * TILE]
+        tile = block[:, :TILE] + jnp.where(row == column, RIDGE, 0.0)
+        if k % 2 == 0:
+            first = tile
+        else:
+            n = (len(TILES) + k // 2) * TILE
+            packed_ref[n : n + TILE, :] = jnp.where(row <= column, first, tile)
+            spare_ref[k // 2 : k // 2 + 1, :] = jnp.sum(
+                jnp.where(row == column, tile, 0.0), axis=0, keepdims=True
+            )
     cross = dot(masked, x, 1, 1)
     half = COLS // 2
-    packed_ref[n * TILE :, :] = jnp.concatenate([cross[:half], cross[half:]], axis=1)
+    n = (len(TILES) + NT // 2) * TILE
+    packed_ref[n:, :] = jnp.concatenate([cross[:half], cross[half:]], axis=1)
 
 
 def factor_tile(d_rows, rows_ref):
@@ -129,16 +136,37 @@
 def fit_kernel(blk_ref, packed_ref, lagged_ref, x_ref, factor_ref, coef_ref, resid_ref, u_ref, w_ref, rows_ref):
     high = lax.Precision.HIGHEST
     half = COLS // 2
-    tiles = {}
-    for n, (k, j) in enumerate(TILES):
-        tiles[k, j] = (n * TILE,)
-    base = len(TILES) * TILE
-    g = {kj: packed_ref[at : at + TILE, :] for kj, (at,) in tiles.items()}
+    devices = COLS // factor_ref.shape[0]
+    share = PACKED // devices
+    pitch = share + SPARE
+
+    def packed_rows(start):
+        pieces, at = [], start
+        while at < start + TILE:
+            stop = min(start + TILE, (at // share + 1) * share)
+            lo = (at // share) * pitch + at % share
+            pieces.append(packed_ref[lo : lo + stop - at, :])
+            at = stop
+        return jnp.concatenate(pieces, axis=0)
+
+    spare = packed_ref[share:pitch, :]
+    for i in range(1, devices):
+        spare = spare + packed_ref[i * pitch + share : (i + 1) * pitch, :]
+    row = lax.broadcasted_iota(jnp.int32, (TILE, TILE), 0)
+    column = lax.broadcasted_iota(jnp.int32, (TILE, TILE), 1)
+    g = {kj: packed_rows(n * TILE) for n, kj in enumerate(TILES)}
+    for k in range(0, NT, 2):
+        both = packed_rows((len(TILES) + k // 2) * TILE)
+        flipped = both.T
+        diagonal = jnp.broadcast_to(spare[k // 2 : k // 2 + 1, :], (TILE, TILE))
+        g[k, k] = jnp.where(row <= column, both, flipped)
+        other = jnp.where(row > column, both, flipped)
+        g[k + 1, k + 1] = jnp.where(row == column, diagonal, other)
+    base = (len(TILES) + NT // 2) * TILE
     b = []
     for k in range(NT):
-        at = base + (k * TILE) % half
         lo = (k * TILE // half) * SENSORS
-        b.append(packed_ref[at : at + TILE, lo : lo + SENSORS])
+        b.append(packed_rows(base + (k * TILE) % half)[:, lo : lo + SENSORS])
     u_ref[...] = jnp.zeros_like(u_ref)
     y = []
     e = {}
@@ -193,14 +221,15 @@
         if b + 1 < blks or g + 1 < grps
     ]
     tail = lax.ppermute(x[:, ROWS - TILE :], ("blk", "grp"), following)
-    lagged, packed = pl.pallas_call(
+    lagged, packed, spare = pl.pallas_call(
         gram_kernel,
         out_shape=[
             jax.ShapeDtypeStruct((COLS, ROWS), BF16),
             jax.ShapeDtypeStruct((PACKED, TILE), F32),
+            jax.ShapeDtypeStruct((SPARE, TILE), F32),
         ],
         in_specs=[SMEM, VMEM, VMEM, VMEM],
-        out_specs=[VMEM, VMEM],
+        out_specs=[VMEM, VMEM, VMEM],
         compiler_params=pltpu.CompilerParams(vmem_limit_bytes=40 << 20),
     )(window_end, lag_table[None, :], tail, x)
 
@@ -217,8 +246,8 @@
     mine = lax.dynamic_index_in_dim(parts, c_index, 1, keepdims=False)
     theirs = lax.dynamic_index_in_dim(parts, 1 - c_index, 1, keepdims=False)
     mine = mine + lax.ppermute(theirs, "blk", other)
-    mine = swap(mine).sum(0)
-    groups = lax.all_to_all(jnp.broadcast_to(mine[None], (grps, share, TILE)), "grp", 0, 0)
+    mine = jnp.concatenate([swap(mine).sum(0), spare], axis=0)
+    groups = lax.all_to_all(jnp.broadcast_to(mine[None], (grps, *mine.shape)), "grp", 0, 0)
     until = (jnp.arange(grps) <= grp)[:, None, None]
     mine = jnp.where(until, groups, 0.0).sum(0)
     prefix = lax.all_gather(mine, "blk", axis=0, tiled=True)

time: 119 us -> 116 us (0.975)
  blocking collectives: 71.8 us -> 69.1 us
    all_to_all x1, blocking collectives: 30.2 us -> 28.4 us  [swap(): return lax.all_to_all(part, 'blk', 0, 0, axis_index_groups=column)]
where the time goes in v5:
time: 116 us
  blocking collectives  69.1 us (60%)
  Pallas kernels  16.8 us (14%)
  starting transfers between devices  14.3 us (12%)
  waiting for transfers between devices  12.4 us (11%)
  local copies, waits for them, and re-layouts  1.61 us (1%)
  between operations  1.39 us (1%)
    all_gather x1, blocking collectives, on_device(): prefix = lax.all_gather(mine, 'blk', axis=0, tiled=True)  40.8 us
    all_to_all x1, blocking collectives, swap(): return lax.all_to_all(part, 'blk', 0, 0, axis_index_groups=column)  28.4 us
    pallas_call x1, Pallas kernels, on_device(): pl.pallas_call(fit_kernel, out_shape=[jax.ShapeDtypeStruct((out_rows, COL...  15.5 us
    all_to_all x1, waiting for transfers between devices, on_device(): lax.all_to_all(jnp.broadcast_to(mine[None], (grps, *mine.shape)), 'grp',...  7.96 us
    all_to_all x1, starting transfers between devices, on_device(): lax.all_to_all(jnp.broadcast_to(mine[None], (grps, *mine.shape)), 'grp',...  6.76 us
    ppermute x1, starting transfers between devices, on_device(): tail = lax.ppermute(x[:, ROWS - TILE:], ('blk', 'grp'), following)  4.92 us
    ppermute x1, waiting for transfers between devices, on_device(): tail = lax.ppermute(x[:, ROWS - TILE:], ('blk', 'grp'), following)  3.21 us
    ppermute x1, starting transfers between devices, on_device(): mine = mine + lax.ppermute(theirs, 'blk', other)  2.59 us
  transfers between devices with their start and end apart: 3, of which 3 were waited for; matrix products, arithmetic and copies ran while one was open for 0% of the time, Pallas kernels for 0%

profile of v5, /device:TPU:1, one launch (start us, length us, event | category | flops | bytes accessed | tf_op | source)
XLA Modules:
  0.0 115.8 jit_solution(1384370843310010822)
XLA Ops:
  0.6 0.0 copy-start
  0.6 0.8 slice.4
  1.4 4.9 %collective-permute-start = (bf16[64,128]{1,0:T(8,128)(2,1)S(1)}, bf16[64,128]{1,0:T(8,128)(2,1)S(1)}, u32[]{:S(2)}, u32[]{:S(2)}) collective-permute-start(bf16[64,128]{1,0:T(8,128)(2,1)S(1)} %slice.4), channel_id=1, source_target_pairs={{0,16},{1,17},{2,18},{3,19},{4,20},{5,21},{6,22},{7,23},{8,24},{9,... | collective-permute-start | bytes 49160 | tf_op jit(solution)/shard_map/ppermute | solution.py:223
  7.0 0.0 copy-start.1
  7.0 3.2 %collective-permute-done.tail_ref = bf16[64,128]{1,0:T(8,128)(2,1)S(1)} collective-permute-done((bf16[64,128]{1,0:T(8,128)(2,1)S(1)}, bf16[64,128]{1,0:T(8,128)(2,1)S(1)}, u32[]{:S(2)}, u32[]{:S(2)}) %collective-permute-start) | collective-permute-done | bytes 16416 | tf_op jit(solution)/shard_map/ppermute | solution.py:223
  10.2 0.0 copy-done
  10.2 0.0 copy-done.1
  10.2 1.3 %shard_map.58 = (bf16[512,512]{1,0:T(8,128)(2,1)S(1)}, f32[1280,128]{1,0:T(8,128)S(1)}, f32[8,128]{1,0:T(8,128)S(1)}) custom-call(s32[1,1]{1,0:T(1,128)S(6)} %copy.6.end_ref, s32[1,512]{1,0:T(1,128)S(1)} %bitcast.16, bf16[64,128]{1,0:T(8,128)(2,1)S(1)} %collective-permute-done.tail_ref, bf16[64,512]{1,0:T(8,128)(2,1)S(1)} %bitcast.14), custom_call_target="tpu_custom_call" | custom-call | tf_op jit(solution)/shard_map/pallas_call | solution.py:224
  11.6 2.6 %collective-permute-start.1 = (f32[16,40,128]{2,1,0:T(8,128)S(1)}, f32[16,40,128]{2,1,0:T(8,128)S(1)}, u32[]{:S(2)}, u32[]{:S(2)}) collective-permute-start(f32[16,40,128]{2,1,0:T(8,128)S(1)} %dynamic-slice_bitcast_fusion), channel_id=1, source_target_pairs={{0,16},{16,0},{32,48},{48,32},{64,80},{80,64},{96,112},{112,96},{1... | collective-permute-start | bytes 983048 | tf_op jit(solution)/shard_map/ppermute | solution.py:248
  14.2 1.2 %collective-permute-done.1 = f32[16,40,128]{2,1,0:T(8,128)S(1)} collective-permute-done((f32[16,40,128]{2,1,0:T(8,128)S(1)}, f32[16,40,128]{2,1,0:T(8,128)S(1)}, u32[]{:S(2)}, u32[]{:S(2)}) %collective-permute-start.1) | collective-permute-done | bytes 327712 | tf_op jit(solution)/shard_map/ppermute | solution.py:248
  15.5 28.4 %all_to_all.10 = f32[16,40,128]{2,1,0:T(8,128)S(1)} all-to-all(f32[16,40,128]{2,1,0:T(8,128)S(1)} %bitcast_add_fusion), channel_id=1, replica_groups={{0,32,64,96,128,160,192,224,256,288,320,352,384,416,448,480},{16,48,80,..., dimensions={0} | all-to-all | bytes 655360 | tf_op jit(solution)/shard_map/all_to_all | solution.py:242
  43.9 0.8 broadcast_in_dim.33
  44.7 6.8 %all-to-all-start.1 = ((f32[16,48,128]{2,1,0:T(8,128)}), f32[16,48,128]{2,1,0:T(8,128)S(1)}, u32[]{:S(2)}, u32[]{:S(2)}) async-start(f32[16,48,128]{2,1,0:T(8,128)} %broadcast_in_dim.33), calls=%async_computation.1 | async-start | bytes 786432 | tf_op jit(solution)/shard_map/all_to_all | solution.py:250
  51.5 8.0 %all-to-all-done.1 = f32[16,48,128]{2,1,0:T(8,128)S(1)} async-done(((f32[16,48,128]{2,1,0:T(8,128)}), f32[16,48,128]{2,1,0:T(8,128)S(1)}, u32[]{:S(2)}, u32[]{:S(2)}) %all-to-all-start.1) | async-done | bytes 393248 | tf_op jit(solution)/shard_map/all_to_all | solution.py:250
  59.4 0.1 select_reduce_fusion
  59.5 40.8 %all_gather.3.packed_ref = f32[1536,128]{1,0:T(8,128)S(1)} all-gather(f32[48,128]{1,0:T(8,128)S(1)} %select_reduce_fusion), channel_id=1, replica_groups=mesh['blk'=32,'grp'=16] {'blk'}, dimensions={0}, use_global_device_ids=true | all-gather | bytes 811008 | tf_op jit(solution)/shard_map/all_gather | solution.py:253
  100.3 15.5 %shard_map.59 = (f32[16,512]{1,0:T(8,128)}, f32[16,64]{1,0:T(8,128)}, f32[64,512]{1,0:T(8,128)}) custom-call(s32[1,1]{1,0:T(1,128)} %bitcast.blk_ref, f32[1536,128]{1,0:T(8,128)S(1)} %all_gather.3.packed_ref, bf16[512,512]{1,0:T(8,128)(2,1)S(1)} %get-tuple-element.11.lagged_ref, bf16[64,512]{1,0:T(8,128)(2,1)S(1)} %bitcast.15), custom_call_target="tpu_custom_call" | custom-call | tf_op jit(solution)/shard_map/pallas_call | solution.py:256
  (5 shorter events, 0.1 us)
Async XLA Ops:
  0.6 9.6 %copy-start = (bf16[1,64,512]{2,1,0:T(8,128)(2,1)S(1)}, bf16[1,64,512]{2,1,0:T(8,128)(2,1)}, u32[]{:S(2)}) copy-start(bf16[1,64,512]{2,1,0:T(8,128)(2,1)} %param.3) | copy-start | bytes 196612
  1.4 8.8 %collective-permute-start = (bf16[64,128]{1,0:T(8,128)(2,1)S(1)}, bf16[64,128]{1,0:T(8,128)(2,1)S(1)}, u32[]{:S(2)}, u32[]{:S(2)}) collective-permute-start(bf16[64,128]{1,0:T(8,128)(2,1)S(1)} %slice.4), channel_id=1, source_target_pairs={{0,16},{1,17},{2,18},{3,19},{4,20},{5,21},{6,22},{7,23},{8,24},{9,... | collective-permute-start | bytes 49160 | tf_op jit(solution)/shard_map/ppermute | solution.py:223
  7.0 3.2 %copy-start.1 = (s32[512]{0:T(512)S(1)}, s32[512]{0:T(512)}, u32[]{:S(2)}) copy-start(s32[512]{0:T(512)} %param.4) | copy-start | bytes 6148
  11.6 3.8 %collective-permute-start.1 = (f32[16,40,128]{2,1,0:T(8,128)S(1)}, f32[16,40,128]{2,1,0:T(8,128)S(1)}, u32[]{:S(2)}, u32[]{:S(2)}) collective-permute-start(f32[16,40,128]{2,1,0:T(8,128)S(1)} %dynamic-slice_bitcast_fusion), channel_id=1, source_target_pairs={{0,16},{16,0},{32,48},{48,32},{64,80},{80,64},{96,112},{112,96},{1... | collective-permute-start | bytes 983048 | tf_op jit(solution)/shard_map/ppermute | solution.py:248
  44.7 14.7 %all-to-all-start.1 = ((f32[16,48,128]{2,1,0:T(8,128)}), f32[16,48,128]{2,1,0:T(8,128)S(1)}, u32[]{:S(2)}, u32[]{:S(2)}) async-start(f32[16,48,128]{2,1,0:T(8,128)} %broadcast_in_dim.33), calls=%async_computation.1 | async-start | bytes 786432 | tf_op jit(solution)/shard_map/all_to_all | solution.py:250

commit v6 on v5

--- a/solution.py
+++ b/solution.py
@@ -27,7 +27,7 @@
     )
 
 
-def gram_kernel(end_ref, table_ref, tail_ref, x_ref, lagged_ref, packed_ref, spare_ref):
+def gram_kernel(end_ref, grp_ref, table_ref, tail_ref, x_ref, lagged_ref, packed_ref, spare_ref, until_ref):
     x = x_ref[...]
     ext = jnp.concatenate([tail_ref[...], x], axis=1).astype(F32)
     pieces = [pltpu.roll(ext, d, 1)[:, TILE:].astype(BF16) for d in range(1, LAGS + 1)]
@@ -41,6 +41,8 @@
     row = lax.broadcasted_iota(jnp.int32, (TILE, TILE), 0)
     column = lax.broadcasted_iota(jnp.int32, (TILE, TILE), 1)
     spare_ref[...] = jnp.zeros_like(spare_ref)
+    group = lax.broadcasted_iota(jnp.int32, until_ref.shape, 0)
+    until_ref[...] = jnp.where(group <= grp_ref[0, 0], 1.0, 0.0)
     for k in range(NT):
         rows = masked[k * TILE : (k + 1) * TILE]
         block = dot(rows, lagged[k * TILE :], 1, 1)
@@ -221,17 +223,18 @@
         if b + 1 < blks or g + 1 < grps
     ]
     tail = lax.ppermute(x[:, ROWS - TILE :], ("blk", "grp"), following)
-    lagged, packed, spare = pl.pallas_call(
+    lagged, packed, spare, until = pl.pallas_call(
         gram_kernel,
         out_shape=[
             jax.ShapeDtypeStruct((COLS, ROWS), BF16),
             jax.ShapeDtypeStruct((PACKED, TILE), F32),
             jax.ShapeDtypeStruct((SPARE, TILE), F32),
+            jax.ShapeDtypeStruct((grps, TILE), F32),
         ],
-        in_specs=[SMEM, VMEM, VMEM, VMEM],
-        out_specs=[VMEM, VMEM, VMEM],
+        in_specs=[SMEM, SMEM, VMEM, VMEM, VMEM],
+        out_specs=[VMEM, VMEM, VMEM, VMEM],
         compiler_params=pltpu.CompilerParams(vmem_limit_bytes=40 << 20),
-    )(window_end, lag_table[None, :], tail, x)
+    )(window_end, grp.reshape(1, 1), lag_table[None, :], tail, x)
 
     core, chips = 2, blks // 2
     column = [[z * core + c for z in range(chips)] for c in range(core)]
@@ -248,8 +251,7 @@
     mine = mine + lax.ppermute(theirs, "blk", other)
     mine = jnp.concatenate([swap(mine).sum(0), spare], axis=0)
     groups = lax.all_to_all(jnp.broadcast_to(mine[None], (grps, *mine.shape)), "grp", 0, 0)
-    until = (jnp.arange(grps) <= grp)[:, None, None]
-    mine = jnp.where(until, groups, 0.0).sum(0)
+    mine = (groups * until[:, None, :]).sum(0)
     prefix = lax.all_gather(mine, "blk", axis=0, tiled=True)
 
     out_rows = COLS // blks

time: 116 us -> 115 us (level)
  blocking collectives: 69.1 us -> 83.7 us
  waiting for transfers between devices: 12.4 us -> 4.44 us
  starting transfers between devices: 14.3 us -> 7.52 us
    all_to_all x0 -> x1, blocking collectives: none -> 14.5 us  [on_device(): lax.all_to_all(jnp.broadcast_to(mine[None], (grps, *mine.shape)), 'grp',...]
    all_to_all x1 -> x0, waiting for transfers between devices: 7.96 us -> none  [on_device(): lax.all_to_all(jnp.broadcast_to(mine[None], (grps, *mine.shape)), 'grp',...]
    all_to_all x1 -> x0, starting transfers between devices: 6.76 us -> none  [on_device(): lax.all_to_all(jnp.broadcast_to(mine[None], (grps, *mine.shape)), 'grp',...]
  transfers between devices with their start and end apart: 3 -> 2, of which waited for: 3 -> 2; matrix products, arithmetic and copies ran while one was open for 0% -> 0% of each run, Pallas kernels for 0% -> 0%
where the time goes in v6:
time: 115 us
  blocking collectives  83.7 us (73%)
  Pallas kernels  16.8 us (15%)
  starting transfers between devices  7.52 us (7%)
  waiting for transfers between devices  4.44 us (4%)
  between operations  1.37 us (1%)
    all_gather x1, blocking collectives, on_device(): prefix = lax.all_gather(mine, 'blk', axis=0, tiled=True)  40.7 us
    all_to_all x1, blocking collectives, swap(): return lax.all_to_all(part, 'blk', 0, 0, axis_index_groups=column)  28.4 us
    pallas_call x1, Pallas kernels, on_device(): pl.pallas_call(fit_kernel, out_shape=[jax.ShapeDtypeStruct((out_rows, COL...  15.5 us
    all_to_all x1, blocking collectives, on_device(): lax.all_to_all(jnp.broadcast_to(mine[None], (grps, *mine.shape)), 'grp',...  14.5 us
    ppermute x1, starting transfers between devices, on_device(): tail = lax.ppermute(x[:, ROWS - TILE:], ('blk', 'grp'), following)  4.92 us
    ppermute x1, waiting for transfers between devices, on_device(): tail = lax.ppermute(x[:, ROWS - TILE:], ('blk', 'grp'), following)  3.21 us
    ppermute x1, starting transfers between devices, on_device(): mine = mine + lax.ppermute(theirs, 'blk', other)  2.6 us
  transfers between devices with their start and end apart: 2, of which 2 were waited for; matrix products, arithmetic and copies ran while one was open for 0% of the time, Pallas kernels for 0%

profile of v6, /device:TPU:1, one launch (start us, length us, event | category | flops | bytes accessed | tf_op | source)
XLA Modules:
  0.0 114.8 jit_solution(15729829728646068060)
XLA Ops:
  0.6 0.0 copy-start
  0.6 0.8 slice.4
  1.4 4.9 %collective-permute-start = (bf16[64,128]{1,0:T(8,128)(2,1)S(1)}, bf16[64,128]{1,0:T(8,128)(2,1)S(1)}, u32[]{:S(2)}, u32[]{:S(2)}) collective-permute-start(bf16[64,128]{1,0:T(8,128)(2,1)S(1)} %slice.4), channel_id=1, source_target_pairs={{0,16},{1,17},{2,18},{3,19},{4,20},{5,21},{6,22},{7,23},{8,24},{9,... | collective-permute-start | bytes 49160 | tf_op jit(solution)/shard_map/ppermute | solution.py:225
  7.0 0.0 copy-start.1
  7.0 3.2 %collective-permute-done.tail_ref = bf16[64,128]{1,0:T(8,128)(2,1)S(1)} collective-permute-done((bf16[64,128]{1,0:T(8,128)(2,1)S(1)}, bf16[64,128]{1,0:T(8,128)(2,1)S(1)}, u32[]{:S(2)}, u32[]{:S(2)}) %collective-permute-start) | collective-permute-done | bytes 16416 | tf_op jit(solution)/shard_map/ppermute | solution.py:225
  10.2 0.0 copy-done
  10.2 0.0 copy-done.1
  10.2 1.3 %shard_map.58 = (bf16[512,512]{1,0:T(8,128)(2,1)S(1)}, f32[1280,128]{1,0:T(8,128)S(1)}, f32[8,128]{1,0:T(8,128)S(1)}, f32[16,128]{1,0:T(8,128)S(1)}) custom-call(s32[1,1]{1,0:T(1,128)S(6)} %copy.6.end_ref, s32[1,1]{1,0:T(1,128)} %bitcast.1.grp_ref, s32[1,512]{1,0:T(1,128)S(1)} %bitcast.17, bf16[64,128]{1,0:T(8,128)(2,1)S(1)} %collective-permute-done.tail_ref, ...), custom_call_target="tpu_custom_call" | custom-call | tf_op jit(solution)/shard_map/pallas_call | solution.py:226
  11.6 2.6 %collective-permute-start.1 = (f32[16,40,128]{2,1,0:T(8,128)S(1)}, f32[16,40,128]{2,1,0:T(8,128)S(1)}, u32[]{:S(2)}, u32[]{:S(2)}) collective-permute-start(f32[16,40,128]{2,1,0:T(8,128)S(1)} %dynamic-slice_bitcast_fusion), channel_id=1, source_target_pairs={{0,16},{16,0},{32,48},{48,32},{64,80},{80,64},{96,112},{112,96},{1... | collective-permute-start | bytes 983048 | tf_op jit(solution)/shard_map/ppermute | solution.py:251
  14.2 1.2 %collective-permute-done.1 = f32[16,40,128]{2,1,0:T(8,128)S(1)} collective-permute-done((f32[16,40,128]{2,1,0:T(8,128)S(1)}, f32[16,40,128]{2,1,0:T(8,128)S(1)}, u32[]{:S(2)}, u32[]{:S(2)}) %collective-permute-start.1) | collective-permute-done | bytes 327712 | tf_op jit(solution)/shard_map/ppermute | solution.py:251
  15.5 28.4 %all_to_all.10 = f32[16,40,128]{2,1,0:T(8,128)S(1)} all-to-all(f32[16,40,128]{2,1,0:T(8,128)S(1)} %bitcast_add_fusion), channel_id=1, replica_groups={{0,32,64,96,128,160,192,224,256,288,320,352,384,416,448,480},{16,48,80,..., dimensions={0} | all-to-all | bytes 655360 | tf_op jit(solution)/shard_map/all_to_all | solution.py:245
  44.0 14.5 %all_to_all.11 = f32[16,48,128]{2,1,0:T(8,128)S(1)} all-to-all(f32[16,48,128]{2,1,0:T(8,128)S(1)} %broadcast_in_dim.20), channel_id=1, replica_groups=mesh['blk'=32,'grp'=16] {'grp'}, dimensions={0} | all-to-all | bytes 786432 | tf_op jit(solution)/shard_map/all_to_all | solution.py:253
  58.6 40.7 %all_gather.3.packed_ref = f32[1536,128]{1,0:T(8,128)S(1)} all-gather(f32[48,128]{1,0:T(8,128)S(1)} %multiply_reduce_fusion), channel_id=1, replica_groups=mesh['blk'=32,'grp'=16] {'blk'}, dimensions={0}, use_global_device_ids=true | all-gather | bytes 811008 | tf_op jit(solution)/shard_map/all_gather | solution.py:255
  99.3 15.5 %shard_map.59 = (f32[16,512]{1,0:T(8,128)}, f32[16,64]{1,0:T(8,128)}, f32[64,512]{1,0:T(8,128)}) custom-call(s32[1,1]{1,0:T(1,128)} %bitcast.blk_ref, f32[1536,128]{1,0:T(8,128)S(1)} %all_gather.3.packed_ref, bf16[512,512]{1,0:T(8,128)(2,1)S(1)} %get-tuple-element.13.lagged_ref, bf16[64,512]{1,0:T(8,128)(2,1)S(1)} %bitcast.16), custom_call_target="tpu_custom_call" | custom-call | tf_op jit(solution)/shard_map/pallas_call | solution.py:258
  (6 shorter events, 0.2 us)
Async XLA Ops:
  0.6 9.6 %copy-start = (bf16[1,64,512]{2,1,0:T(8,128)(2,1)S(1)}, bf16[1,64,512]{2,1,0:T(8,128)(2,1)}, u32[]{:S(2)}) copy-start(bf16[1,64,512]{2,1,0:T(8,128)(2,1)} %param.3) | copy-start | bytes 196612
  1.4 8.8 %collective-permute-start = (bf16[64,128]{1,0:T(8,128)(2,1)S(1)}, bf16[64,128]{1,0:T(8,128)(2,1)S(1)}, u32[]{:S(2)}, u32[]{:S(2)}) collective-permute-start(bf16[64,128]{1,0:T(8,128)(2,1)S(1)} %slice.4), channel_id=1, source_target_pairs={{0,16},{1,17},{2,18},{3,19},{4,20},{5,21},{6,22},{7,23},{8,24},{9,... | collective-permute-start | bytes 49160 | tf_op jit(solution)/shard_map/ppermute | solution.py:225
  7.0 3.2 %copy-start.1 = (s32[512]{0:T(512)S(1)}, s32[512]{0:T(512)}, u32[]{:S(2)}) copy-start(s32[512]{0:T(512)} %param.4) | copy-start | bytes 6148
  11.6 3.8 %collective-permute-start.1 = (f32[16,40,128]{2,1,0:T(8,128)S(1)}, f32[16,40,128]{2,1,0:T(8,128)S(1)}, u32[]{:S(2)}, u32[]{:S(2)}) collective-permute-start(f32[16,40,128]{2,1,0:T(8,128)S(1)} %dynamic-slice_bitcast_fusion), channel_id=1, source_target_pairs={{0,16},{16,0},{32,48},{48,32},{64,80},{80,64},{96,112},{112,96},{1... | collective-permute-start | bytes 983048 | tf_op jit(solution)/shard_map/ppermute | solution.py:251

commit v7 on v6

--- a/solution.py
+++ b/solution.py
@@ -68,8 +68,8 @@
     n = len(d_rows)
     lane = lax.broadcasted_iota(jnp.int32, (8, TILE), 1)
     sub = lax.broadcasted_iota(jnp.int32, (8, TILE), 0)
-    d = list(d_rows)
-    x = [jnp.where(lane == 8 * q + sub, 1.0, 0.0) for q in range(n)]
+    m = list(d_rows)
+    d, x = [], []
 
     def col(v, c):
         return jnp.broadcast_to(v[:, c : c + 1], (8, TILE))
@@ -80,6 +80,7 @@
 
     for p in range(n):
         base = 8 * p
+        pivot = (lane >= base) & (lane < base + 8)
 
         def rows_of(v, slot, count):
             at = 8 * (slot + 10 * (p % 2))
@@ -88,12 +89,14 @@
 
         s = {}
         for j in range(8):
-            for i, v in enumerate(rows_of(col(d[p], base + j), j, j + 1)):
+            for i, v in enumerate(rows_of(col(m[p], base + j), j, j + 1)):
                 s[i, j] = v
-        r = rows_of(d[p], 8, 8)
-        xr = rows_of(x[p], 9, 8)
-        cn = [col(d[p + 1], base + j) for j in range(8)] if p + 1 < n else []
-        sets = [v for v in (r, xr, cn) if v]
+        r = rows_of(jnp.where(pivot, jnp.where(lane == base + sub, 1.0, 0.0), m[p]), 8, 8)
+        cols = {q: [col(m[q], base + j) for j in range(8)] for q in range(p + 1, n)}
+        for q in range(p + 1, n):
+            m[q] = jnp.where(pivot, 0.0, m[q])
+        cn = list(cols[p + 1]) if p + 1 < n else []
+        sets = [r, cn] if cn else [r]
         u, inv = {}, [None] * 8
         for k in range(0, 8, 2):
             one, off, two = s[k, k], s[k, k + 1], s[k + 1, k + 1]
@@ -101,6 +104,8 @@
             w1 = lax.rsqrt((one * two - off * off) * one) * one
             inv[k], inv[k + 1] = w0, w1
             u[k, k + 1] = off * w0
+            u[k, k] = one * w0
+            u[k + 1, k + 1] = (two - u[k, k + 1] * u[k, k + 1]) * w1
             for j in range(k + 2, 8):
                 u[k, j] = s[k, j] * w0
                 u[k + 1, j] = (s[k + 1, j] - u[k, k + 1] * u[k, j]) * w1
@@ -113,25 +118,26 @@
                 for i in range(k + 2, 8):
                     v[i] = (v[i] - u[k, i] * v[k]) - u[k + 1, i] * v[k + 1]
         if p + 1 < n:
-            d[p + 1] = less(d[p + 1], cn, r)
-            x[p + 1] = less(x[p + 1], cn, xr)
+            m[p + 1] = less(m[p + 1], cn, r)
         if p + 2 < n:
-            z, xz = list(r), list(xr)
+            z = list(r)
             for k in reversed(range(8)):
-                for v in (z, xz):
-                    v[k] = v[k] * inv[k]
-                    for i in range(k):
-                        v[i] = v[i] - u[i, k] * v[k]
+                z[k] = z[k] * inv[k]
+                for i in range(k):
+                    z[i] = z[i] - u[i, k] * z[k]
             for q in range(p + 2, n):
-                cq = [col(d[q], base + j) for j in range(8)]
-                d[q] = less(d[q], cq, z)
-                x[q] = less(x[q], cq, xz)
-        du, dx = r[0], xr[0]
+                m[q] = less(m[q], cols[q], z)
+        both = r[0]
         for i in range(1, 8):
-            du = jnp.where(sub == i, r[i], du)
-            dx = jnp.where(sub == i, xr[i], dx)
-        d[p] = jnp.where(lane >= base + sub, du, 0.0)
-        x[p] = dx
+            both = jnp.where(sub == i, r[i], both)
+        corner = jnp.zeros((8, TILE), F32)
+        for j in range(8):
+            v = u[0, j]
+            for i in range(1, j + 1):
+                v = jnp.where(sub == i, u[i, j], v)
+            corner = jnp.where((lane == base + j) & (sub <= j), v, corner)
+        d.append(jnp.where(lane >= base + 8, both, corner))
+        x.append(jnp.where(lane < base + 8, both, 0.0))
     return d, x
 
 
@@ -178,16 +184,19 @@
         xkk = jnp.concatenate(xi, axis=0)
         u_ref[k * TILE : (k + 1) * TILE, k * TILE : (k + 1) * TILE] = ukk
         panel = {}
+        e[k, k] = xkk
         for j in range(k + 1, NT):
             panel[j] = dot(xkk, g[k, j], 1, 0, high)
+            if j == k + 1:
+                g[j, j] = g[j, j] - dot(panel[j], panel[j], 0, 0, high)
             u_ref[k * TILE : (k + 1) * TILE, j * TILE : (j + 1) * TILE] = panel[j]
         y.append(dot(xkk, b[k], 1, 0, high))
-        e[k, k] = xkk
         for i in range(k):
             e[k, i] = dot(xkk, e[k, i], 1, 0, high)
         for i in range(k + 1, NT):
             for j in range(i, NT):
-                g[i, j] = g[i, j] - dot(panel[i], panel[j], 0, 0, high)
+                if (i, j) != (k + 1, k + 1):
+                    g[i, j] = g[i, j] - dot(panel[i], panel[j], 0, 0, high)
             b[i] = b[i] - dot(panel[i], y[k], 0, 0, high)
             for h in range(k + 1):
                 past = dot(panel[i], e[k, h], 0, 0, high)

time: 115 us -> 115 us (level)
  no operation moved by 1% of the time
where the time goes in v7:
time: 115 us
  blocking collectives  83.7 us (73%)
  Pallas kernels  16.5 us (14%)
  starting transfers between devices  7.52 us (7%)
  waiting for transfers between devices  4.44 us (4%)
  between operations  1.37 us (1%)
    all_gather x1, blocking collectives, on_device(): prefix = lax.all_gather(mine, 'blk', axis=0, tiled=True)  40.7 us
    all_to_all x1, blocking collectives, swap(): return lax.all_to_all(part, 'blk', 0, 0, axis_index_groups=column)  28.4 us
    pallas_call x1, Pallas kernels, on_device(): pl.pallas_call(fit_kernel, out_shape=[jax.ShapeDtypeStruct((out_rows, COL...  15.2 us
    all_to_all x1, blocking collectives, on_device(): lax.all_to_all(jnp.broadcast_to(mine[None], (grps, *mine.shape)), 'grp',...  14.5 us
    ppermute x1, starting transfers between devices, on_device(): tail = lax.ppermute(x[:, ROWS - TILE:], ('blk', 'grp'), following)  4.92 us
    ppermute x1, waiting for transfers between devices, on_device(): tail = lax.ppermute(x[:, ROWS - TILE:], ('blk', 'grp'), following)  3.21 us
    ppermute x1, starting transfers between devices, on_device(): mine = mine + lax.ppermute(theirs, 'blk', other)  2.6 us
  transfers between devices with their start and end apart: 2, of which 2 were waited for; matrix products, arithmetic and copies ran while one was open for 0% of the time, Pallas kernels for 0%

profile of v7, /device:TPU:1, one launch (start us, length us, event | category | flops | bytes accessed | tf_op | source)
XLA Modules:
  0.0 114.5 jit_solution(9095201740654299888)
XLA Ops:
  0.6 0.0 copy-start
  0.6 0.8 slice.4
  1.4 4.9 %collective-permute-start = (bf16[64,128]{1,0:T(8,128)(2,1)S(1)}, bf16[64,128]{1,0:T(8,128)(2,1)S(1)}, u32[]{:S(2)}, u32[]{:S(2)}) collective-permute-start(bf16[64,128]{1,0:T(8,128)(2,1)S(1)} %slice.4), channel_id=1, source_target_pairs={{0,16},{1,17},{2,18},{3,19},{4,20},{5,21},{6,22},{7,23},{8,24},{9,... | collective-permute-start | bytes 49160 | tf_op jit(solution)/shard_map/ppermute | solution.py:234
  7.0 0.0 copy-start.1
  7.0 3.2 %collective-permute-done.tail_ref = bf16[64,128]{1,0:T(8,128)(2,1)S(1)} collective-permute-done((bf16[64,128]{1,0:T(8,128)(2,1)S(1)}, bf16[64,128]{1,0:T(8,128)(2,1)S(1)}, u32[]{:S(2)}, u32[]{:S(2)}) %collective-permute-start) | collective-permute-done | bytes 16416 | tf_op jit(solution)/shard_map/ppermute | solution.py:234
  10.2 0.0 copy-done
  10.2 0.0 copy-done.1
  10.2 1.3 %shard_map.58 = (bf16[512,512]{1,0:T(8,128)(2,1)S(1)}, f32[1280,128]{1,0:T(8,128)S(1)}, f32[8,128]{1,0:T(8,128)S(1)}, f32[16,128]{1,0:T(8,128)S(1)}) custom-call(s32[1,1]{1,0:T(1,128)S(6)} %copy.6.end_ref, s32[1,1]{1,0:T(1,128)} %bitcast.1.grp_ref, s32[1,512]{1,0:T(1,128)S(1)} %bitcast.17, bf16[64,128]{1,0:T(8,128)(2,1)S(1)} %collective-permute-done.tail_ref, ...), custom_call_target="tpu_custom_call" | custom-call | tf_op jit(solution)/shard_map/pallas_call | solution.py:235
  11.6 2.6 %collective-permute-start.1 = (f32[16,40,128]{2,1,0:T(8,128)S(1)}, f32[16,40,128]{2,1,0:T(8,128)S(1)}, u32[]{:S(2)}, u32[]{:S(2)}) collective-permute-start(f32[16,40,128]{2,1,0:T(8,128)S(1)} %dynamic-slice_bitcast_fusion), channel_id=1, source_target_pairs={{0,16},{16,0},{32,48},{48,32},{64,80},{80,64},{96,112},{112,96},{1... | collective-permute-start | bytes 983048 | tf_op jit(solution)/shard_map/ppermute | solution.py:260
  14.2 1.2 %collective-permute-done.1 = f32[16,40,128]{2,1,0:T(8,128)S(1)} collective-permute-done((f32[16,40,128]{2,1,0:T(8,128)S(1)}, f32[16,40,128]{2,1,0:T(8,128)S(1)}, u32[]{:S(2)}, u32[]{:S(2)}) %collective-permute-start.1) | collective-permute-done | bytes 327712 | tf_op jit(solution)/shard_map/ppermute | solution.py:260
  15.5 28.4 %all_to_all.10 = f32[16,40,128]{2,1,0:T(8,128)S(1)} all-to-all(f32[16,40,128]{2,1,0:T(8,128)S(1)} %bitcast_add_fusion), channel_id=1, replica_groups={{0,32,64,96,128,160,192,224,256,288,320,352,384,416,448,480},{16,48,80,..., dimensions={0} | all-to-all | bytes 655360 | tf_op jit(solution)/shard_map/all_to_all | solution.py:254
  44.0 14.5 %all_to_all.11 = f32[16,48,128]{2,1,0:T(8,128)S(1)} all-to-all(f32[16,48,128]{2,1,0:T(8,128)S(1)} %broadcast_in_dim.20), channel_id=1, replica_groups=mesh['blk'=32,'grp'=16] {'grp'}, dimensions={0} | all-to-all | bytes 786432 | tf_op jit(solution)/shard_map/all_to_all | solution.py:262
  58.6 40.7 %all_gather.3.packed_ref = f32[1536,128]{1,0:T(8,128)S(1)} all-gather(f32[48,128]{1,0:T(8,128)S(1)} %multiply_reduce_fusion), channel_id=1, replica_groups=mesh['blk'=32,'grp'=16] {'blk'}, dimensions={0}, use_global_device_ids=true | all-gather | bytes 811008 | tf_op jit(solution)/shard_map/all_gather | solution.py:264
  99.3 15.2 %shard_map.59 = (f32[16,512]{1,0:T(8,128)}, f32[16,64]{1,0:T(8,128)}, f32[64,512]{1,0:T(8,128)}) custom-call(s32[1,1]{1,0:T(1,128)} %bitcast.blk_ref, f32[1536,128]{1,0:T(8,128)S(1)} %all_gather.3.packed_ref, bf16[512,512]{1,0:T(8,128)(2,1)S(1)} %get-tuple-element.13.lagged_ref, bf16[64,512]{1,0:T(8,128)(2,1)S(1)} %bitcast.16), custom_call_target="tpu_custom_call" | custom-call | tf_op jit(solution)/shard_map/pallas_call | solution.py:267
  (6 shorter events, 0.2 us)
Async XLA Ops:
  0.6 9.6 %copy-start = (bf16[1,64,512]{2,1,0:T(8,128)(2,1)S(1)}, bf16[1,64,512]{2,1,0:T(8,128)(2,1)}, u32[]{:S(2)}) copy-start(bf16[1,64,512]{2,1,0:T(8,128)(2,1)} %param.3) | copy-start | bytes 196612
  1.4 8.8 %collective-permute-start = (bf16[64,128]{1,0:T(8,128)(2,1)S(1)}, bf16[64,128]{1,0:T(8,128)(2,1)S(1)}, u32[]{:S(2)}, u32[]{:S(2)}) collective-permute-start(bf16[64,128]{1,0:T(8,128)(2,1)S(1)} %slice.4), channel_id=1, source_target_pairs={{0,16},{1,17},{2,18},{3,19},{4,20},{5,21},{6,22},{7,23},{8,24},{9,... | collective-permute-start | bytes 49160 | tf_op jit(solution)/shard_map/ppermute | solution.py:234
  7.0 3.2 %copy-start.1 = (s32[512]{0:T(512)S(1)}, s32[512]{0:T(512)}, u32[]{:S(2)}) copy-start(s32[512]{0:T(512)} %param.4) | copy-start | bytes 6148
  11.6 3.8 %collective-permute-start.1 = (f32[16,40,128]{2,1,0:T(8,128)S(1)}, f32[16,40,128]{2,1,0:T(8,128)S(1)}, u32[]{:S(2)}, u32[]{:S(2)}) collective-permute-start(f32[16,40,128]{2,1,0:T(8,128)S(1)} %dynamic-slice_bitcast_fusion), channel_id=1, source_target_pairs={{0,16},{16,0},{32,48},{48,32},{64,80},{80,64},{96,112},{112,96},{1... | collective-permute-start | bytes 983048 | tf_op jit(solution)/shard_map/ppermute | solution.py:260

commit v8 on v7

--- a/solution.py
+++ b/solution.py
@@ -185,22 +185,29 @@
         u_ref[k * TILE : (k + 1) * TILE, k * TILE : (k + 1) * TILE] = ukk
         panel = {}
         e[k, k] = xkk
+        if k + 1 < NT:
+            panel[k + 1] = dot(xkk, g[k, k + 1], 1, 0, high)
+            g[k + 1, k + 1] = g[k + 1, k + 1] - dot(panel[k + 1], panel[k + 1], 0, 0, high)
+        wide = [g[k, j] for j in range(k + 2, NT)] + [e[k, i] for i in range(k)] + [b[k]]
+        solved = dot(xkk, jnp.concatenate(wide, axis=1), 1, 0, high)
+        for n, j in enumerate(range(k + 2, NT)):
+            panel[j] = solved[:, n * TILE : (n + 1) * TILE]
+        at = max(NT - k - 2, 0)
+        for i in range(k):
+            e[k, i] = solved[:, (at + i) * TILE : (at + i + 1) * TILE]
+        y.append(solved[:, (at + k) * TILE :])
         for j in range(k + 1, NT):
-            panel[j] = dot(xkk, g[k, j], 1, 0, high)
-            if j == k + 1:
-                g[j, j] = g[j, j] - dot(panel[j], panel[j], 0, 0, high)
             u_ref[k * TILE : (k + 1) * TILE, j * TILE : (j + 1) * TILE] = panel[j]
-        y.append(dot(xkk, b[k], 1, 0, high))
-        for i in range(k):
-            e[k, i] = dot(xkk, e[k, i], 1, 0, high)
         for i in range(k + 1, NT):
-            for j in range(i, NT):
-                if (i, j) != (k + 1, k + 1):
-                    g[i, j] = g[i, j] - dot(panel[i], panel[j], 0, 0, high)
-            b[i] = b[i] - dot(panel[i], y[k], 0, 0, high)
+            js = [j for j in range(i, NT) if (i, j) != (k + 1, k + 1)]
+            wide = [panel[j] for j in js] + [e[k, h] for h in range(k + 1)] + [y[k]]
+            past = dot(panel[i], jnp.concatenate(wide, axis=1), 0, 0, high)
+            for n, j in enumerate(js):
+                g[i, j] = g[i, j] - past[:, n * TILE : (n + 1) * TILE]
             for h in range(k + 1):
-                past = dot(panel[i], e[k, h], 0, 0, high)
-                e[i, h] = e[i, h] - past if (i, h) in e else -past
+                part = past[:, (len(js) + h) * TILE : (len(js) + h + 1) * TILE]
+                e[i, h] = e[i, h] - part if (i, h) in e else -part
+            b[i] = b[i] - past[:, (len(js) + k + 1) * TILE :]
     for k in range(NT):
         acc = dot(e[k, k], y[k], 0, 0, high)
         for j in range(k + 1, NT):

time: 115 us -> 115 us (level)
  no operation moved by 1% of the time
where the time goes in v8:
time: 115 us; the launch traced here: 114 us
  blocking collectives  83.7 us (73%)
  Pallas kernels  16.4 us (14%)
  starting transfers between devices  7.52 us (7%)
  waiting for transfers between devices  4.44 us (4%)
  between operations  1.37 us (1%)
    all_gather x1, blocking collectives, on_device(): prefix = lax.all_gather(mine, 'blk', axis=0, tiled=True)  40.7 us
    all_to_all x1, blocking collectives, swap(): return lax.all_to_all(part, 'blk', 0, 0, axis_index_groups=column)  28.4 us
    pallas_call x1, Pallas kernels, on_device(): pl.pallas_call(fit_kernel, out_shape=[jax.ShapeDtypeStruct((out_rows, COL...  15.1 us
    all_to_all x1, blocking collectives, on_device(): lax.all_to_all(jnp.broadcast_to(mine[None], (grps, *mine.shape)), 'grp',...  14.5 us
    ppermute x1, starting transfers between devices, on_device(): tail = lax.ppermute(x[:, ROWS - TILE:], ('blk', 'grp'), following)  4.92 us
    ppermute x1, waiting for transfers between devices, on_device(): tail = lax.ppermute(x[:, ROWS - TILE:], ('blk', 'grp'), following)  3.21 us
    ppermute x1, starting transfers between devices, on_device(): mine = mine + lax.ppermute(theirs, 'blk', other)  2.6 us
  transfers between devices with their start and end apart: 2, of which 2 were waited for; matrix products, arithmetic and copies ran while one was open for 0% of the time, Pallas kernels for 0%

profile of v8, /device:TPU:1, one launch (start us, length us, event | category | flops | bytes accessed | tf_op | source)
XLA Modules:
  0.0 114.3 jit_solution(6438667367917323973)
XLA Ops:
  0.6 0.0 copy-start
  0.6 0.8 slice.4
  1.4 4.9 %collective-permute-start = (bf16[64,128]{1,0:T(8,128)(2,1)S(1)}, bf16[64,128]{1,0:T(8,128)(2,1)S(1)}, u32[]{:S(2)}, u32[]{:S(2)}) collective-permute-start(bf16[64,128]{1,0:T(8,128)(2,1)S(1)} %slice.4), channel_id=1, source_target_pairs={{0,16},{1,17},{2,18},{3,19},{4,20},{5,21},{6,22},{7,23},{8,24},{9,... | collective-permute-start | bytes 49160 | tf_op jit(solution)/shard_map/ppermute | solution.py:241
  7.0 0.0 copy-start.1
  7.0 3.2 %collective-permute-done.tail_ref = bf16[64,128]{1,0:T(8,128)(2,1)S(1)} collective-permute-done((bf16[64,128]{1,0:T(8,128)(2,1)S(1)}, bf16[64,128]{1,0:T(8,128)(2,1)S(1)}, u32[]{:S(2)}, u32[]{:S(2)}) %collective-permute-start) | collective-permute-done | bytes 16416 | tf_op jit(solution)/shard_map/ppermute | solution.py:241
  10.2 0.0 copy-done
  10.2 0.0 copy-done.1
  10.2 1.3 %shard_map.58 = (bf16[512,512]{1,0:T(8,128)(2,1)S(1)}, f32[1280,128]{1,0:T(8,128)S(1)}, f32[8,128]{1,0:T(8,128)S(1)}, f32[16,128]{1,0:T(8,128)S(1)}) custom-call(s32[1,1]{1,0:T(1,128)S(6)} %copy.6.end_ref, s32[1,1]{1,0:T(1,128)} %bitcast.1.grp_ref, s32[1,512]{1,0:T(1,128)S(1)} %bitcast.17, bf16[64,128]{1,0:T(8,128)(2,1)S(1)} %collective-permute-done.tail_ref, ...), custom_call_target="tpu_custom_call" | custom-call | tf_op jit(solution)/shard_map/pallas_call | solution.py:242
  11.6 2.6 %collective-permute-start.1 = (f32[16,40,128]{2,1,0:T(8,128)S(1)}, f32[16,40,128]{2,1,0:T(8,128)S(1)}, u32[]{:S(2)}, u32[]{:S(2)}) collective-permute-start(f32[16,40,128]{2,1,0:T(8,128)S(1)} %dynamic-slice_bitcast_fusion), channel_id=1, source_target_pairs={{0,16},{16,0},{32,48},{48,32},{64,80},{80,64},{96,112},{112,96},{1... | collective-permute-start | bytes 983048 | tf_op jit(solution)/shard_map/ppermute | solution.py:267
  14.2 1.2 %collective-permute-done.1 = f32[16,40,128]{2,1,0:T(8,128)S(1)} collective-permute-done((f32[16,40,128]{2,1,0:T(8,128)S(1)}, f32[16,40,128]{2,1,0:T(8,128)S(1)}, u32[]{:S(2)}, u32[]{:S(2)}) %collective-permute-start.1) | collective-permute-done | bytes 327712 | tf_op jit(solution)/shard_map/ppermute | solution.py:267
  15.5 28.4 %all_to_all.10 = f32[16,40,128]{2,1,0:T(8,128)S(1)} all-to-all(f32[16,40,128]{2,1,0:T(8,128)S(1)} %bitcast_add_fusion), channel_id=1, replica_groups={{0,32,64,96,128,160,192,224,256,288,320,352,384,416,448,480},{16,48,80,..., dimensions={0} | all-to-all | bytes 655360 | tf_op jit(solution)/shard_map/all_to_all | solution.py:261
  44.0 14.5 %all_to_all.11 = f32[16,48,128]{2,1,0:T(8,128)S(1)} all-to-all(f32[16,48,128]{2,1,0:T(8,128)S(1)} %broadcast_in_dim.20), channel_id=1, replica_groups=mesh['blk'=32,'grp'=16] {'grp'}, dimensions={0} | all-to-all | bytes 786432 | tf_op jit(solution)/shard_map/all_to_all | solution.py:269
  58.6 40.7 %all_gather.3.packed_ref = f32[1536,128]{1,0:T(8,128)S(1)} all-gather(f32[48,128]{1,0:T(8,128)S(1)} %multiply_reduce_fusion), channel_id=1, replica_groups=mesh['blk'=32,'grp'=16] {'blk'}, dimensions={0}, use_global_device_ids=true | all-gather | bytes 811008 | tf_op jit(solution)/shard_map/all_gather | solution.py:271
  99.3 15.1 %shard_map.59 = (f32[16,512]{1,0:T(8,128)}, f32[16,64]{1,0:T(8,128)}, f32[64,512]{1,0:T(8,128)}) custom-call(s32[1,1]{1,0:T(1,128)} %bitcast.blk_ref, f32[1536,128]{1,0:T(8,128)S(1)} %all_gather.3.packed_ref, bf16[512,512]{1,0:T(8,128)(2,1)S(1)} %get-tuple-element.13.lagged_ref, bf16[64,512]{1,0:T(8,128)(2,1)S(1)} %bitcast.16), custom_call_target="tpu_custom_call" | custom-call | tf_op jit(solution)/shard_map/pallas_call | solution.py:274
  (6 shorter events, 0.2 us)
Async XLA Ops:
  0.6 9.6 %copy-start = (bf16[1,64,512]{2,1,0:T(8,128)(2,1)S(1)}, bf16[1,64,512]{2,1,0:T(8,128)(2,1)}, u32[]{:S(2)}) copy-start(bf16[1,64,512]{2,1,0:T(8,128)(2,1)} %param.3) | copy-start | bytes 196612
  1.4 8.8 %collective-permute-start = (bf16[64,128]{1,0:T(8,128)(2,1)S(1)}, bf16[64,128]{1,0:T(8,128)(2,1)S(1)}, u32[]{:S(2)}, u32[]{:S(2)}) collective-permute-start(bf16[64,128]{1,0:T(8,128)(2,1)S(1)} %slice.4), channel_id=1, source_target_pairs={{0,16},{1,17},{2,18},{3,19},{4,20},{5,21},{6,22},{7,23},{8,24},{9,... | collective-permute-start | bytes 49160 | tf_op jit(solution)/shard_map/ppermute | solution.py:241
  7.0 3.2 %copy-start.1 = (s32[512]{0:T(512)S(1)}, s32[512]{0:T(512)}, u32[]{:S(2)}) copy-start(s32[512]{0:T(512)} %param.4) | copy-start | bytes 6148
  11.6 3.8 %collective-permute-start.1 = (f32[16,40,128]{2,1,0:T(8,128)S(1)}, f32[16,40,128]{2,1,0:T(8,128)S(1)}, u32[]{:S(2)}, u32[]{:S(2)}) collective-permute-start(f32[16,40,128]{2,1,0:T(8,128)S(1)} %dynamic-slice_bitcast_fusion), channel_id=1, source_target_pairs={{0,16},{16,0},{32,48},{48,32},{64,80},{80,64},{96,112},{112,96},{1... | collective-permute-start | bytes 983048 | tf_op jit(solution)/shard_map/ppermute | solution.py:267
